TPU v7x, 32 devices: a whole 2x2x4 slice. The times are simulated.
32 devices in a mesh: dp: 8 (over z, x), mp: 4 (over y, core).
Axes of the slice: x: 2, y: 2, z: 4, core: 2. Of those that a mesh axis runs over, the one named last changes fastest.
Arguments:
- new_rows: bfloat16 [256, 8, 4, 1536], P(None, 'dp', None, 'mp'), may hold values from -50 to 50
- counts: int32 [8], replicated, may hold values from 1 to 640, 2048 in all
- history_len: int32 [8], replicated, may hold values from 1 to 512, as said below
- user_owner: int32 [8], replicated, may hold values from 0 to 7, each once
- cache_kv: bfloat16 [8, 512, 2, 1536], P('dp', None, None, 'mp'), may hold values from -50 to 50
- w_out: bfloat16 [1536, 1536], P(None, 'mp'), may hold values from -0.15625 to 0.15625
Outputs:
- new_kv: bfloat16 [8, 640, 2, 1536], P('dp', None, None, 'mp')
- layer_out: bfloat16 [8, 640, 1536], P('dp', None, 'mp')
Inputs may be any that keep to these rules, and one draw needn't show every extreme that they name: `counts`: each user has at least one new event, 2048 in all; some user has exactly 640. `history_len`: some user has exactly 512. `user_owner`: A permutation of the cache slots.
All inputs are finite; a program needn't handle non-finite values.
Results may differ from a plain program's by a relative error of at most 0.0057.
Values may be sent and summed in bfloat16 or wider, within the bound.
A program may use at most 64 MiB of HBM per device.

v0:
```python
import math

import jax
import jax.numpy as jnp
from jax import lax
from jax.sharding import PartitionSpec as P

DH = 128
CAP = 640


EPSILON = 1e-06


def normalize(attended, gate_rows, width_all):
    total_sum, total_squares = lax.psum(
        (jnp.sum(attended, axis=-1), jnp.sum(attended * attended, axis=-1)), "mp"
    )
    row_mean = total_sum / width_all
    row_var = total_squares / width_all - row_mean * row_mean
    normed = (attended - row_mean[:, None]) * lax.rsqrt(row_var + EPSILON)[:, None]
    return (normed * gate_rows.astype(jnp.float32)).astype(jnp.bfloat16)


def project(gated, w_out):
    return jnp.dot(
        lax.all_gather(gated, "mp", axis=1, tiled=True), w_out, preferred_element_type=jnp.float32
    )


def per_device(new_rows, counts, history_len, user_owner, cache_kv, w_out):
    dp_count = lax.axis_size("dp")
    my_index = lax.axis_index("dp")
    local_rows = new_rows.shape[0]
    per_peer = CAP // dp_count
    width_all = w_out.shape[0]
    user_ids = jnp.arange(counts.shape[0], dtype=jnp.int32)
    starts = jnp.cumsum(counts) - counts
    event_ids = jnp.arange(local_rows, dtype=jnp.int32) * dp_count + my_index
    row_user = jnp.sum((starts[None, :] <= event_ids[:, None]).astype(jnp.int32), axis=1) - 1
    one_hot = (user_ids[None, :] == row_user[:, None]).astype(jnp.int32)
    row_first = jnp.sum(one_hot * starts[None, :], axis=1)
    row_owner = jnp.sum(one_hot * user_owner[None, :], axis=1)
    position = (event_ids - row_first) // dp_count * dp_count + row_owner
    is_mine = (user_owner == my_index).astype(jnp.int32)
    new_count = jnp.sum(counts * is_mine)
    first_row = jnp.sum(starts * is_mine)
    history = jnp.sum(history_len * is_mine)
    is_live = jnp.arange(CAP, dtype=jnp.int32) < new_count
    event_rows = new_rows[:, 0]
    feature_here = event_rows.shape[-1]
    heads_here = feature_here // DH
    history_cap = cache_kv.shape[1]
    cache_keys = cache_kv[0, :, 0].reshape(history_cap, heads_here, DH)
    cache_values = cache_kv[0, :, 1].reshape(history_cap, heads_here, DH)
    score_scale = 1.0 / math.sqrt(DH)
    buffer = jnp.zeros((CAP,) + event_rows.shape[1:], event_rows.dtype).at[position].set(event_rows)
    arrived = lax.all_to_all(
        buffer.reshape((per_peer, dp_count) + event_rows.shape[1:]),
        "dp",
        split_axis=1,
        concat_axis=1,
        tiled=True,
    )
    ordered = jnp.roll(arrived, -first_row, axis=1).reshape((CAP,) + arrived.shape[2:])
    queries = ordered[:, 0].reshape(CAP, heads_here, DH)
    own_keys = ordered[:, 1].reshape(CAP, heads_here, DH)
    own_values = ordered[:, 2].reshape(CAP, heads_here, DH)
    scores = (
        jnp.einsum("ehd,jhd->hej", queries, cache_keys, preferred_element_type=jnp.float32)
        * score_scale
    )
    visible = jnp.arange(history_cap, dtype=jnp.int32) < history
    weights = jnp.where(visible[None, None, :], jax.nn.silu(scores), 0.0).astype(jnp.bfloat16)
    summed = jnp.einsum("hej,jhd->ehd", weights, cache_values, preferred_element_type=jnp.float32)
    own_score = (
        jnp.sum(queries.astype(jnp.float32) * own_keys.astype(jnp.float32), axis=-1) * score_scale
    )
    attended = (summed + jax.nn.silu(own_score)[:, :, None] * own_values.astype(jnp.float32)) / (
        history + 1
    ).astype(jnp.float32)
    attended = attended.reshape(CAP, feature_here)
    gated = normalize(attended, ordered[:, 3], width_all)
    mixed_rows = project(gated, w_out)
    results = jnp.where(is_live[:, None], mixed_rows, 0.0).astype(jnp.bfloat16)
    key_value = ordered[:, 1:3]
    return (key_value[None], results[None])


def solution(mesh):
    placed = (P(None, "dp", None, "mp"), P(), P(), P(), P("dp", None, None, "mp"), P(None, "mp"))
    return jax.shard_map(
        per_device,
        mesh=mesh,
        in_specs=placed,
        out_specs=(P("dp", None, None, "mp"), P("dp", None, "mp")),
        check_vma=False,
    )
```

profile of v0, /device:TPU:11, one launch (start us, length us, event | category | flops | bytes accessed | tf_op | source)
XLA Modules:
  0.0 143.6 jit_solution(13997677350066719827)
XLA Ops:
  7.2 0.0 copy-start
  7.2 0.9 reduce-window.9
  8.1 1.4 select_reduce_fusion.3
  9.5 0.1 convert_reduce_fusion
  9.6 0.7 select_reduce_fusion.1
  10.3 0.5 broadcast_in_dim.30
  10.8 19.6 %scatter_fusion = bf16[640,4,384]{2,1,0:T(4,128)(2,1)S(1)} fusion(bf16[640,4,384]{2,1,0:T(4,128)(2,1)S(1)} %broadcast_in_dim.30, s32[256]{0:T(256)S(1)} %bitcast.46, bf16[256,4,384]{2,1,0:T(4,128)(2,1)} %bitcast.43), kind=kCustom, calls=%fused_computation | custom fusion | bytes 2360320 | tf_op jit(solution)/shard_map/scatter | solution.py:57
  30.4 2.0 %copy.40 = bf16[80,8,4,384]{3,0,2,1:T(8,128)(2,1)} copy(bf16[80,8,4,384]{3,2,1,0:T(4,128)(2,1)S(1)} %bitcast.37) | data formatting | bytes 3932160 | tf_op jit(solution)/shard_map/reshape | solution.py:59
  32.4 5.7 %all-to-all-start = ((bf16[80,8,4,384]{3,0,2,1:T(8,128)(2,1)}), bf16[80,8,4,384]{3,0,2,1:T(8,128)(2,1)S(1)}, u32[]{:S(2)}, u32[]{:S(2)}) async-start(bf16[80,8,4,384]{3,0,2,1:T(8,128)(2,1)} %copy.40), calls=%async_computation | async-start | bytes 3932160 | tf_op jit(solution)/shard_map/all_to_all | solution.py:58
  38.0 0.0 all-gather.2.cloned.1.call-start
  40.0 3.9 %fusion.13 = (bf16[1,512,1,384]{3,2,1,0:T(2,128)(2,1)}, bf16[1,512,1,384]{3,2,1,0:T(2,128)(2,1)}) fusion(bf16[1,512,2,384]{3,2,1,0:T(2,128)(2,1)} %param.10), kind=kLoop, calls=%fused_computation.46 | loop fusion | bytes 1572864 | tf_op jit(solution)/shard_map/slice | solution.py:54
  43.9 2.2 %copy.56 = bf16[1,512,1,384]{1,3,2,0:T(8,128)(2,1)S(1)} copy(bf16[1,512,1,384]{3,2,1,0:T(2,128)(2,1)} %get-tuple-element.23) | data formatting | bytes 786432
  46.1 2.9 %copy.47 = bf16[1,512,1,384]{1,3,2,0:T(8,128)(2,1)} copy(bf16[1,512,1,384]{3,2,1,0:T(2,128)(2,1)} %get-tuple-element.24) | data formatting | bytes 786432 | tf_op jit(solution)/shard_map/slice | solution.py:55
  49.0 1.2 iota_compare_fusion.2
  50.2 30.7 %all-to-all-done = bf16[80,8,4,384]{3,0,2,1:T(8,128)(2,1)S(1)} async-done(((bf16[80,8,4,384]{3,0,2,1:T(8,128)(2,1)}), bf16[80,8,4,384]{3,0,2,1:T(8,128)(2,1)S(1)}, u32[]{:S(2)}, u32[]{:S(2)}) %all-to-all-start) | async-done | bytes 1966112 | tf_op jit(solution)/shard_map/all_to_all | solution.py:58
  80.9 1.1 copy.41
  82.1 1.4 fusion.1
  83.5 1.5 %slice_convert_fusion.1 = (f32[640,1,384]{2,0,1:T(8,128)}, f32[640,1,384]{2,0,1:T(8,128)}, bf16[640,1,384]{2,0,1:T(8,128)(2,1)}) fusion(bf16[640,4,384]{2,0,1:T(8,128)(2,1)S(1)} %fusion.1), kind=kLoop, calls=%fused_computation.20 | loop fusion | flops 491520 | bytes 3932160 | tf_op jit(solution)/shard_map/convert_element_type | solution.py:77
  85.0 2.5 %copy.48 = f32[640,1,384]{0,2,1:T(8,128)} copy(f32[640,1,384]{2,0,1:T(8,128)} %get-tuple-element.20) | data formatting | bytes 1966080 | tf_op jit(solution)/shard_map/convert_element_type | solution.py:77
  87.5 2.0 %copy.43 = bf16[640,1,384]{0,2,1:T(8,128)(2,1)} copy(bf16[640,1,384]{2,0,1:T(8,128)(2,1)} %get-tuple-element.22) | data formatting | bytes 983040 | tf_op jit(solution)/shard_map/slice | solution.py:66
  89.5 1.4 %multiply_reduce_fusion.1 = f32[640,3]{0,1:T(4,128)S(1)} fusion(f32[640,3,128]{0,2,1:T(8,128)} %bitcast.38, bf16[640,3,128]{0,2,1:T(8,128)(2,1)} %bitcast.39), kind=kLoop, calls=%fused_computation.16 | loop fusion | flops 735360 | bytes 1482240 | tf_op jit(solution)/shard_map/reduce_sum | solution.py:77
  91.0 2.5 %copy.49 = f32[640,1,384]{0,2,1:T(8,128)} copy(f32[640,1,384]{2,0,1:T(8,128)} %get-tuple-element.21) | data formatting | bytes 1966080 | tf_op jit(solution)/shard_map/convert_element_type | solution.py:79
  93.5 4.9 %fusion.12 = (f32[640]{0:T(1024)S(1)}, f32[640]{0:T(1024)}, f32[640,3,128]{0,2,1:T(8,128)}) fusion(f32[]{:T(128)S(6)} %convert_element_type.53, f32[640,3,128]{0,2,1:T(8,128)} %bitcast.41, f32[640,3]{0,1:T(4,128)S(1)} %divide_multiply_fusion, bf16[512,3,128]{0,2,1:T(8,128)(2,1)} %bitcast.45, bf16[640,3,128]{0,2,1:T(8,128)(2,1)} %bitcast.40, ...), kind=kOutput, calls=%fused_computation.45 | convolution fusion | flops 511671040 | bytes 3257348 | tf_op jit(solution)/shard_map/hej,jhd->ehd/dot_general | solution.py:75
  98.4 0.0 copy-start.1
  98.4 2.5 %copy.50 = f32[640,384]{1,0:T(8,128)} copy(f32[640,384]{0,1:T(8,128)} %bitcast.42) | data formatting | bytes 1966080 | tf_op jit(solution)/shard_map/reshape | solution.py:82
  100.9 0.0 copy-done.1
  100.9 5.6 %all-reduce = (f32[640]{0:T(1024)S(1)}, f32[640]{0:T(1024)S(1)}) all-reduce(f32[640]{0:T(1024)S(1)} %copy-done.1, f32[640]{0:T(1024)S(1)} %get-tuple-element.10), channel_id=1, replica_groups=mesh['dp'=8,'mp'=4] {'mp'}, use_global_device_ids=true, to_apply=%region_12.13 | all-reduce | flops 1280 | bytes 10240 | tf_op jit(solution)/shard_map/psum | solution.py:16
  106.5 2.2 %fusion.7 = bf16[640,384]{1,0:T(8,128)(2,1)} fusion(f32[640,384]{1,0:T(8,128)} %copy.50, bf16[640,4,384]{2,0,1:T(8,128)(2,1)S(1)} %fusion.1, f32[640]{0:T(1024)S(1)} %get-tuple-element.26, f32[640]{0:T(1024)S(1)} %get-tuple-element.25), kind=kLoop, calls=%fused_computation.14 | loop fusion | flops 1228800 | bytes 1971200 | tf_op jit(solution)/shard_map/convert_element_type | solution.py:22
  108.8 0.0 all-gather.2.cloned.1.call-update
  108.8 0.5 iota_compare_fusion.1
  109.3 0.1 slice_bitcast_fusion
  109.4 2.0 %copy.51 = bf16[1,640,2,384]{3,2,1,0:T(2,128)(2,1)} copy(bf16[1,640,2,384]{3,1,2,0:T(8,128)(2,1)S(1)} %slice_bitcast_fusion) | data formatting | bytes 1966080
  111.4 21.9 %all-gather.2.cloned.1.call-done = bf16[640,1536]{1,0:T(8,128)(2,1)} async-done(((bf16[640,384]{1,0:T(8,128)(2,1)}), bf16[640,1536]{1,0:T(8,128)(2,1)}) %all-gather.2.cloned.1.call-update) | async-done | bytes 1966096 | tf_op jit(solution)/shard_map/all_gather | solution.py:27
  133.3 0.0 copy-done
  133.3 3.5 %fusion.6 = bf16[1,640,384]{2,1,0:T(8,128)(2,1)} fusion(bf16[640,1536]{1,0:T(8,128)(2,1)} %all-gather.2.cloned.1.call-done, bf16[1536,384]{1,0:T(8,128)(2,1)S(1)} %copy-done, pred[640]{0:T(1024)(128)(4,1)S(1)} %iota_compare_fusion.1), kind=kOutput, calls=%fused_computation.11 | convolution fusion | flops 755466240 | bytes 3637888 | tf_op jit(solution)/shard_map/dot_general | solution.py:26
  (5 shorter events, 0.1 us)
Async XLA Ops:
  7.2 126.1 %copy-start = (bf16[1536,384]{1,0:T(8,128)(2,1)S(1)}, bf16[1536,384]{1,0:T(8,128)(2,1)}, u32[]{:S(2)}) copy-start(bf16[1536,384]{1,0:T(8,128)(2,1)} %param.11) | copy-start | bytes 3538948
  32.4 48.6 %all-to-all-start = ((bf16[80,8,4,384]{3,0,2,1:T(8,128)(2,1)}), bf16[80,8,4,384]{3,0,2,1:T(8,128)(2,1)S(1)}, u32[]{:S(2)}, u32[]{:S(2)}) async-start(bf16[80,8,4,384]{3,0,2,1:T(8,128)(2,1)} %copy.40), calls=%async_computation | async-start | bytes 3932160 | tf_op jit(solution)/shard_map/all_to_all | solution.py:58
  38.0 95.3 %all-gather.2.cloned.1.call-start = ((), (), s32[]{:S(2)}) async-start(), calls=%async_computation.1 | async-start | bytes 2457600 | tf_op jit(solution)/shard_map/all_gather | solution.py:27
  98.4 2.5 %copy-start.1 = (f32[640]{0:T(1024)S(1)}, f32[640]{0:T(1024)}, u32[]{:S(2)}) copy-start(f32[640]{0:T(1024)} %get-tuple-element.11) | copy-start | bytes 7684
Sparse Core Ops, SparseCore 0:
  108.9 24.3 all-gather.1
where the time goes:
time: 146 us; the launch traced here: 144 us
  waiting for transfers between devices  52.6 us (36%)
  local copies, waits for them, and re-layouts  43.8 us (30%)
  between operations  16.1 us (11%)
  other arithmetic  11.5 us (8%)
  matrix products  8.45 us (6%)
  starting transfers between devices  5.66 us (4%)
  blocking collectives  5.55 us (4%)
    all_to_all x1, waiting for transfers between devices, per_device(): lax.all_to_all(buffer.reshape((per_peer, dp_count) + event_rows.shape[1:]...  30.7 us
    all_gather x1, waiting for transfers between devices, project(): lax.all_gather(gated, 'mp', axis=1, tiled=True)  21.9 us
    scatter x1, local copies, waits for them, and re-layouts, per_device(): jnp.zeros((CAP,) + event_rows.shape[1:], event_rows.dtype).at[position]  19.6 us
    all_to_all x1, starting transfers between devices, per_device(): lax.all_to_all(buffer.reshape((per_peer, dp_count) + event_rows.shape[1:]...  5.66 us
    psum x1, blocking collectives, normalize(): lax.psum((jnp.sum(attended, axis=-1), jnp.sum(attended * attended, axis=-...  5.55 us
    dot_general x1, matrix products, per_device(): jnp.einsum('hej,jhd->ehd', weights, cache_values, preferred_element_type=...  4.95 us
    unnamed x6, local copies, waits for them, and re-layouts  4.15 us
    slice x1, local copies, waits for them, and re-layouts, per_device(): cache_keys = cache_kv[0, :, 0].reshape(history_cap, heads_here, DH)  3.93 us
  transfers between devices with their start and end apart: 2, of which 2 were waited for; matrix products, arithmetic and copies ran while one was open for 9% of the time, Pallas kernels for 0%

commit v1 on v0

--- a/solution.py
+++ b/solution.py
@@ -1,12 +1,16 @@
+import functools
 import math
 
 import jax
 import jax.numpy as jnp
 from jax import lax
+from jax.experimental import pallas as pl
+from jax.experimental.pallas import tpu as pltpu
 from jax.sharding import PartitionSpec as P
 
 DH = 128
 CAP = 640
+TILE = 16
 
 
 EPSILON = 1e-06
@@ -28,7 +32,7 @@
     )
 
 
-def per_device(new_rows, counts, history_len, user_owner, cache_kv, w_out):
+def general_device(new_rows, counts, history_len, user_owner, cache_kv, w_out):
     dp_count = lax.axis_size("dp")
     my_index = lax.axis_index("dp")
     local_rows = new_rows.shape[0]
@@ -87,10 +91,286 @@
     return (key_value[None], results[None])
 
 
+def half_silu(half):
+    return half + half * jnp.tanh(half)
+
+
+def layer_kernel(
+    dp_count,
+    mp_count,
+    counts_ref,
+    history_ref,
+    owner_ref,
+    rows_ref,
+    cache_ref,
+    w_ref,
+    kv_ref,
+    out_ref,
+    send_buf,
+    recv_buf,
+    values_buf,
+    perm_buf,
+    attended_buf,
+    gate_buf,
+    stats_buf,
+    gated_buf,
+    row_send,
+    row_recv,
+    stats_send,
+    stats_recv,
+    gated_send,
+    gated_recv,
+):
+    me = lax.axis_index("dp")
+    my_part = lax.axis_index("mp")
+    users = counts_ref.shape[0]
+    local_rows = rows_ref.shape[0]
+    width = w_ref.shape[1]
+    width_all = w_ref.shape[0]
+    heads = width // DH
+    history_cap = cache_ref.shape[0]
+    chunks = send_buf.shape[0]
+    chunk = dp_count * TILE
+    half_scale = 0.5 / math.sqrt(DH)
+
+    def peer(step):
+        return lax.rem(me + step, dp_count)
+
+    def part(step):
+        return lax.rem(my_part + step, mp_count)
+
+    def row_copy(c, source, target):
+        return pltpu.make_async_remote_copy(
+            src_ref=send_buf.at[c, target],
+            dst_ref=recv_buf.at[c, source],
+            send_sem=row_send.at[c, target],
+            recv_sem=row_recv.at[c, source],
+            device_id=(target, my_part),
+            device_id_type=pl.DeviceIdType.MESH,
+        )
+
+    def part_copy(buf, send_sem, recv_sem, c, source, target):
+        return pltpu.make_async_remote_copy(
+            src_ref=buf.at[c, source],
+            dst_ref=buf.at[c, source],
+            send_sem=send_sem.at[c, target],
+            recv_sem=recv_sem.at[c, source],
+            device_id=(me, target),
+            device_id_type=pl.DeviceIdType.MESH,
+        )
+
+    barrier = pltpu.get_barrier_semaphore()
+    for step in range(1, dp_count):
+        pl.semaphore_signal(
+            barrier, inc=1, device_id=(peer(step), my_part), device_id_type=pl.DeviceIdType.MESH
+        )
+    for step in range(1, mp_count):
+        pl.semaphore_signal(
+            barrier, inc=1, device_id=(me, part(step)), device_id_type=pl.DeviceIdType.MESH
+        )
+
+    slot_first = [jnp.int32(0)] * dp_count
+    my_count = jnp.int32(0)
+    my_first = jnp.int32(0)
+    my_history = jnp.int32(0)
+    first = jnp.int32(0)
+    for user in range(users):
+        count = counts_ref[user]
+        owner = owner_ref[user]
+        slot_first = [
+            jnp.where(owner == slot, first, slot_first[slot]) for slot in range(dp_count)
+        ]
+        mine = owner == me
+        my_count = jnp.where(mine, count, my_count)
+        my_first = jnp.where(mine, first, my_first)
+        my_history = jnp.where(mine, history_ref[user], my_history)
+        first = first + count
+    slot_row = [lax.div(value - me + (dp_count - 1), dp_count) for value in slot_first]
+
+    row_id = lax.broadcasted_iota(jnp.int32, (TILE, local_rows), 1)
+    tile_id = lax.broadcasted_iota(jnp.int32, (TILE, local_rows), 0)
+    offset = row_id - tile_id
+
+    pl.semaphore_wait(barrier, dp_count - 1 + mp_count - 1)
+
+    def pack(c, carry):
+        picked = jnp.concatenate(
+            [
+                jnp.where(offset == slot_row[slot] + c * TILE, 1.0, 0.0).astype(jnp.bfloat16)
+                for slot in range(dp_count)
+            ],
+            axis=0,
+        )
+        sent = jnp.dot(picked, rows_ref[...], preferred_element_type=jnp.float32)
+        send_buf[c] = sent.astype(jnp.bfloat16).reshape(dp_count, TILE, 4 * width)
+        for step in range(1, dp_count):
+            row_copy(c, me, peer(step)).start()
+        recv_buf[c, me] = send_buf[c, me]
+        return carry
+
+    lax.fori_loop(0, chunks, pack, 0)
+
+    place = lax.broadcasted_iota(jnp.int32, (chunk, chunk), 0)
+    landed = lax.broadcasted_iota(jnp.int32, (chunk, chunk), 1)
+    source_of = landed // TILE
+    ordered_at = dp_count * (landed - source_of * TILE) + lax.rem(
+        source_of - lax.rem(my_first, dp_count) + dp_count, dp_count
+    )
+    perm_buf[...] = jnp.where(place == ordered_at, 1.0, 0.0).astype(jnp.bfloat16)
+    history_id = lax.broadcasted_iota(jnp.int32, (history_cap, width), 0)
+    values_buf[...] = jnp.where(
+        history_id < my_history, cache_ref[:, width:].astype(jnp.float32), 0.0
+    ).astype(jnp.bfloat16)
+    lane = lax.broadcasted_iota(jnp.int32, (chunk, 128), 1)
+    chunk_row = lax.broadcasted_iota(jnp.int32, (chunk, 1), 0)
+    inverse = 1.0 / (my_history + 1).astype(jnp.float32)
+
+    def attend(c):
+        for step in range(1, dp_count):
+            row_copy(c, peer(step), me).wait_recv()
+        arrived = recv_buf[c].reshape(chunk, 4 * width)
+        ordered = jnp.dot(perm_buf[...], arrived, preferred_element_type=jnp.float32)
+        here = pl.ds(pl.multiple_of(c * chunk, chunk), chunk)
+        live = c * chunk + chunk_row < my_count
+        kv_ref[here, :] = jnp.where(live, ordered[:, width : 3 * width], 0.0).astype(jnp.bfloat16)
+        gate_buf[...] = ordered[:, 3 * width :]
+        total = jnp.zeros((chunk, 1), jnp.float32)
+        squares = jnp.zeros((chunk, 1), jnp.float32)
+        for head in range(heads):
+            columns = slice(head * DH, (head + 1) * DH)
+            query = ordered[:, columns]
+            key = ordered[:, width + head * DH : width + (head + 1) * DH]
+            value = ordered[:, 2 * width + head * DH : 2 * width + (head + 1) * DH]
+            half = (
+                lax.dot_general(
+                    query.astype(jnp.bfloat16),
+                    cache_ref[:, columns],
+                    (((1,), (1,)), ((), ())),
+                    preferred_element_type=jnp.float32,
+                )
+                * half_scale
+            )
+            summed = jnp.dot(
+                half_silu(half).astype(jnp.bfloat16),
+                values_buf[:, columns],
+                preferred_element_type=jnp.float32,
+            )
+            own = jnp.sum(query * key, axis=1, keepdims=True) * half_scale
+            attended = (summed + half_silu(own) * value) * inverse
+            attended_buf[:, columns] = attended
+            total = total + jnp.sum(attended, axis=1, keepdims=True)
+            squares = squares + jnp.sum(attended * attended, axis=1, keepdims=True)
+        both = jnp.where(lane == 0, total, jnp.where(lane == 1, squares, 0.0))
+        stats_buf[c, my_part] = both.T[:8]
+        for step in range(1, mp_count):
+            part_copy(stats_buf, stats_send, stats_recv, c, my_part, part(step)).start()
+
+    def gate(c):
+        for step in range(1, mp_count):
+            part_copy(stats_buf, stats_send, stats_recv, c, part(step), my_part).wait_recv()
+        stats = stats_buf[c, 0]
+        for index in range(1, mp_count):
+            stats = stats + stats_buf[c, index]
+        stats = jnp.concatenate([stats, jnp.zeros((128 - 8, chunk), jnp.float32)], axis=0).T
+        mean = stats[:, 0:1] / width_all
+        variance = stats[:, 1:2] / width_all - mean * mean
+        normed = (attended_buf[...] - mean) * lax.rsqrt(variance + EPSILON)
+        gated_buf[c, my_part] = (normed * gate_buf[...]).astype(jnp.bfloat16)
+        for step in range(1, mp_count):
+            part_copy(gated_buf, gated_send, gated_recv, c, my_part, part(step)).start()
+
+    def mix(c):
+        for step in range(1, mp_count):
+            part_copy(gated_buf, gated_send, gated_recv, c, part(step), my_part).wait_recv()
+        mixed = jnp.zeros((chunk, width), jnp.float32)
+        for index in range(mp_count):
+            mixed = mixed + jnp.dot(
+                gated_buf[c, index],
+                w_ref[index * width : (index + 1) * width, :],
+                preferred_element_type=jnp.float32,
+            )
+        here = pl.ds(pl.multiple_of(c * chunk, chunk), chunk)
+        live = c * chunk + chunk_row < my_count
+        out_ref[here, :] = jnp.where(live, mixed, 0.0).astype(jnp.bfloat16)
+
+    def work(c, carry):
+        attend(c)
+
+        @pl.when(c > 0)
+        def _():
+            mix(c - 1)
+
+        gate(c)
+        return carry
+
+    lax.fori_loop(0, chunks, work, 0)
+    mix(chunks - 1)
+
+    def finish(c, carry):
+        for step in range(1, dp_count):
+            row_copy(c, me, peer(step)).wait_send()
+        for step in range(1, mp_count):
+            part_copy(stats_buf, stats_send, stats_recv, c, my_part, part(step)).wait_send()
+            part_copy(gated_buf, gated_send, gated_recv, c, my_part, part(step)).wait_send()
+        return carry
+
+    lax.fori_loop(0, chunks, finish, 0)
+
+
+def kernel_device(new_rows, counts, history_len, user_owner, cache_kv, w_out):
+    dp_count = lax.axis_size("dp")
+    mp_count = lax.axis_size("mp")
+    width = w_out.shape[1]
+    local_rows = new_rows.shape[0]
+    history_cap = cache_kv.shape[1]
+    chunks = CAP // (dp_count * TILE)
+    chunk = dp_count * TILE
+    smem = pl.BlockSpec(memory_space=pltpu.SMEM)
+    vmem = pl.BlockSpec(memory_space=pltpu.VMEM)
+    dma = pltpu.SemaphoreType.DMA
+    key_value, results = pl.pallas_call(
+        functools.partial(layer_kernel, dp_count, mp_count),
+        out_shape=(
+            jax.ShapeDtypeStruct((CAP, 2 * width), jnp.bfloat16),
+            jax.ShapeDtypeStruct((CAP, width), jnp.bfloat16),
+        ),
+        in_specs=[smem, smem, smem, vmem, vmem, vmem],
+        out_specs=(vmem, vmem),
+        scratch_shapes=[
+            pltpu.VMEM((chunks, dp_count, TILE, 4 * width), jnp.bfloat16),
+            pltpu.VMEM((chunks, dp_count, TILE, 4 * width), jnp.bfloat16),
+            pltpu.VMEM((history_cap, width), jnp.bfloat16),
+            pltpu.VMEM((chunk, chunk), jnp.bfloat16),
+            pltpu.VMEM((chunk, width), jnp.float32),
+            pltpu.VMEM((chunk, width), jnp.float32),
+            pltpu.VMEM((chunks, mp_count, 8, chunk), jnp.float32),
+            pltpu.VMEM((chunks, mp_count, chunk, width), jnp.bfloat16),
+            dma((chunks, dp_count)),
+            dma((chunks, dp_count)),
+            dma((chunks, mp_count)),
+            dma((chunks, mp_count)),
+            dma((chunks, mp_count)),
+            dma((chunks, mp_count)),
+        ],
+        compiler_params=pltpu.CompilerParams(
+            collective_id=0, has_side_effects=True, vmem_limit_bytes=40 * 2**20
+        ),
+    )(
+        counts,
+        history_len,
+        user_owner,
+        new_rows.reshape(local_rows, 4 * width),
+        cache_kv.reshape(history_cap, 2 * width),
+        w_out,
+    )
+    return (key_value.reshape(1, CAP, 2, width), results[None])
+
+
 def solution(mesh):
     placed = (P(None, "dp", None, "mp"), P(), P(), P(), P("dp", None, None, "mp"), P(None, "mp"))
+    fits = mesh.shape["dp"] * TILE == 128
     return jax.shard_map(
-        per_device,
+        kernel_device if fits else general_device,
         mesh=mesh,
         in_specs=placed,
         out_specs=(P("dp", None, None, "mp"), P("dp", None, "mp")),

time: 146 us -> 71.9 us (0.49); the launches traced: 144 us -> 71.7 us
  Pallas kernels: 0 us -> 66.5 us
  waiting for transfers between devices: 52.6 us -> 0 us
  local copies, waits for them, and re-layouts: 43.8 us -> 4.5 us
  between operations: 16.1 us -> 0.7 us
  other arithmetic: 11.5 us -> 0 us
  matrix products: 8.45 us -> 0 us
  starting transfers between devices: 5.66 us -> 0 us
  blocking collectives: 5.55 us -> 0 us
    pallas_call x0 -> x1, Pallas kernels: none -> 66.5 us  [kernel_device(): pl.pallas_call(functools.partial(layer_kernel, dp_count, mp_count), out_s...]
    all_to_all x1 -> x0, waiting for transfers between devices: 30.7 us -> none  [per_device(): lax.all_to_all(buffer.reshape((per_peer, dp_count) + event_rows.shape[1:]...]
    all_gather x1 -> x0, waiting for transfers between devices: 21.9 us -> none  [project(): lax.all_gather(gated, 'mp', axis=1, tiled=True)]
    scatter x1 -> x0, local copies, waits for them, and re-layouts: 19.6 us -> none  [per_device(): jnp.zeros((CAP,) + event_rows.shape[1:], event_rows.dtype).at[position]]
    slice x3 -> x0, local copies, waits for them, and re-layouts: 8.85 us -> none  [the longest x1 3.93 us: per_device(): cache_keys = cache_kv[0, :, 0].reshape(history_cap, heads_here, DH)]
    dot_general x2 -> x0, matrix products: 8.45 us -> none  [the longest x1 4.95 us: per_device(): jnp.einsum('hej,jhd->ehd', weights, cache_values, preferred_element_type=...]
    all_to_all x1 -> x0, starting transfers between devices: 5.66 us -> none  [per_device(): lax.all_to_all(buffer.reshape((per_peer, dp_count) + event_rows.shape[1:]...]
    psum x1 -> x0, blocking collectives: 5.55 us -> none  [normalize(): lax.psum((jnp.sum(attended, axis=-1), jnp.sum(attended * attended, axis=-...]
  transfers between devices with their start and end apart: 2 -> 0, of which waited for: 2 -> 0; matrix products, arithmetic and copies ran while one was open for 9% -> 0% of each run, Pallas kernels for 0% -> 0%
where the time goes in v1:
time: 71.9 us; the launch traced here: 71.7 us
  Pallas kernels  66.5 us (92%)
  local copies, waits for them, and re-layouts  4.5 us (6%)
    pallas_call x1, Pallas kernels, kernel_device(): pl.pallas_call(functools.partial(layer_kernel, dp_count, mp_count), out_s...  66.5 us
    unnamed x13, local copies, waits for them, and re-layouts  3.33 us

profile of v1, /device:TPU:11, one launch (start us, length us, event | category | flops | bytes accessed | tf_op | source)
XLA Modules:
  0.0 71.7 jit_solution(6740060672186546011)
XLA Ops:
  0.6 0.0 copy-start.4
  0.6 1.3 %copy.8 = bf16[32,8,4,384]{3,1,2,0:T(8,128)(2,1)S(1)} copy(bf16[32,8,4,384]{3,2,1,0:T(4,128)(2,1)} %bitcast.10) | data formatting | bytes 1572864
  2.0 0.0 copy-start
  2.0 0.0 copy-start.1
  2.0 0.0 copy-start.2
  2.0 0.0 copy-start.3
  2.0 0.0 copy-done.4
  2.0 0.1 copy.9
  2.1 1.1 %copy-done = bf16[1536,384]{1,0:T(8,128)(2,1)S(1)} copy-done((bf16[1536,384]{1,0:T(8,128)(2,1)S(1)}, bf16[1536,384]{1,0:T(8,128)(2,1)}, u32[]{:S(2)}) %copy-start) | copy-done | bytes 1179672
  3.2 0.0 copy-done.1
  3.2 0.0 copy-done.2
  3.2 0.0 copy-done.3
  3.2 66.5 %shard_map.77 = (bf16[640,768]{1,0:T(8,128)(2,1)S(1)}, bf16[640,384]{1,0:T(8,128)(2,1)S(1)}) custom-call(s32[8]{0:T(128)S(1)} %copy-done.1, s32[8]{0:T(128)S(1)} %copy-done.2, s32[8]{0:T(128)S(1)} %copy-done.3, bf16[256,1536]{1,0:T(8,128)(2,1)S(1)} %bitcast.7, bf16[512,768]{1,0:T(8,128)(2,1)S(1)} %bitcast.8, bf16[1536,384]{1,0:T(8,128)(2,1)S(1)} %copy-done), custom_call_target="tpu_custom_call" | custom-call | tf_op jit(solution)/shard_map/pallas_call | solution.py:331
  69.8 1.2 %reshape.15 = bf16[1,640,2,384]{3,2,1,0:T(2,128)(2,1)} reshape(bf16[640,768]{1,0:T(8,128)(2,1)S(1)} %get-tuple-element.4) | data formatting | bytes 1966080 | tf_op jit(solution)/shard_map/reshape | solution.py:366
  70.9 0.8 %copy.11 = bf16[1,640,384]{2,1,0:T(8,128)(2,1)} copy(bf16[1,640,384]{2,1,0:T(8,128)(2,1)S(1)} %bitcast.9) | data formatting | bytes 983040
Async XLA Ops:
  0.6 1.4 %copy-start.4 = (bf16[1,512,2,384]{3,2,1,0:T(2,128)(2,1)S(1)}, bf16[1,512,2,384]{3,2,1,0:T(2,128)(2,1)}, u32[]{:S(2)}) copy-start(bf16[1,512,2,384]{3,2,1,0:T(2,128)(2,1)} %param.10) | copy-start | bytes 2359300
  2.0 1.3 %copy-start = (bf16[1536,384]{1,0:T(8,128)(2,1)S(1)}, bf16[1536,384]{1,0:T(8,128)(2,1)}, u32[]{:S(2)}) copy-start(bf16[1536,384]{1,0:T(8,128)(2,1)} %w_ref.1) | copy-start | bytes 3538948
  2.0 1.3 %copy-start.1 = (s32[8]{0:T(128)S(1)}, s32[8]{0:T(128)}, u32[]{:S(2)}) copy-start(s32[8]{0:T(128)} %counts_ref.1) | copy-start | bytes 100
  2.0 1.3 %copy-start.2 = (s32[8]{0:T(128)S(1)}, s32[8]{0:T(128)}, u32[]{:S(2)}) copy-start(s32[8]{0:T(128)} %history_ref.1) | copy-start | bytes 100
  2.0 1.3 %copy-start.3 = (s32[8]{0:T(128)S(1)}, s32[8]{0:T(128)}, u32[]{:S(2)}) copy-start(s32[8]{0:T(128)} %owner_ref.1) | copy-start | bytes 100

commit v2 on v1

--- a/solution.py
+++ b/solution.py
@@ -11,6 +11,7 @@
 DH = 128
 CAP = 640
 TILE = 16
+EVENTS = 8
 
 
 EPSILON = 1e-06
@@ -106,6 +107,7 @@
     w_ref,
     kv_ref,
     out_ref,
+    w_buf,
     send_buf,
     recv_buf,
     values_buf,
@@ -120,7 +122,10 @@
     stats_recv,
     gated_send,
     gated_recv,
+    w_sem,
 ):
+    fetch_w = pltpu.make_async_copy(w_ref, w_buf, w_sem)
+    fetch_w.start()
     me = lax.axis_index("dp")
     my_part = lax.axis_index("mp")
     users = counts_ref.shape[0]
@@ -130,7 +135,7 @@
     heads = width // DH
     history_cap = cache_ref.shape[0]
     chunks = send_buf.shape[0]
-    chunk = dp_count * TILE
+    chunk = dp_count * EVENTS
     half_scale = 0.5 / math.sqrt(DH)
 
     def peer(step):
@@ -189,29 +194,40 @@
 
     row_id = lax.broadcasted_iota(jnp.int32, (TILE, local_rows), 1)
     tile_id = lax.broadcasted_iota(jnp.int32, (TILE, local_rows), 0)
-    offset = row_id - tile_id
-
-    pl.semaphore_wait(barrier, dp_count - 1 + mp_count - 1)
-
-    def pack(c, carry):
+    offset = row_id - lax.rem(tile_id, EVENTS)
+    upper = lax.broadcasted_iota(jnp.int32, (dp_count, TILE, 2 * width), 1) < EVENTS
+
+    def pack(c):
         picked = jnp.concatenate(
             [
-                jnp.where(offset == slot_row[slot] + c * TILE, 1.0, 0.0).astype(jnp.bfloat16)
+                jnp.where(offset == slot_row[slot] + c * EVENTS, 1.0, 0.0).astype(jnp.bfloat16)
                 for slot in range(dp_count)
             ],
             axis=0,
         )
         sent = jnp.dot(picked, rows_ref[...], preferred_element_type=jnp.float32)
-        send_buf[c] = sent.astype(jnp.bfloat16).reshape(dp_count, TILE, 4 * width)
+        sent = sent.reshape(dp_count, TILE, 4 * width)
+        send_buf[c] = jnp.where(upper, sent[:, :, : 2 * width], sent[:, :, 2 * width :]).astype(
+            jnp.bfloat16
+        )
+
+    def post(c):
         for step in range(1, dp_count):
             row_copy(c, me, peer(step)).start()
         recv_buf[c, me] = send_buf[c, me]
+
+    def pack_and_post(c, carry):
+        pack(c)
+        post(c)
         return carry
 
-    lax.fori_loop(0, chunks, pack, 0)
-
-    place = lax.broadcasted_iota(jnp.int32, (chunk, chunk), 0)
-    landed = lax.broadcasted_iota(jnp.int32, (chunk, chunk), 1)
+    pack(0)
+    pl.semaphore_wait(barrier, dp_count - 1 + mp_count - 1)
+    post(0)
+    lax.fori_loop(1, chunks, pack_and_post, 0)
+
+    place = lax.broadcasted_iota(jnp.int32, (2 * chunk, 2 * chunk), 0)
+    landed = lax.broadcasted_iota(jnp.int32, (2 * chunk, 2 * chunk), 1)
     source_of = landed // TILE
     ordered_at = dp_count * (landed - source_of * TILE) + lax.rem(
         source_of - lax.rem(my_first, dp_count) + dp_count, dp_count
@@ -228,19 +244,21 @@
     def attend(c):
         for step in range(1, dp_count):
             row_copy(c, peer(step), me).wait_recv()
-        arrived = recv_buf[c].reshape(chunk, 4 * width)
+        arrived = recv_buf[c].reshape(2 * chunk, 2 * width)
         ordered = jnp.dot(perm_buf[...], arrived, preferred_element_type=jnp.float32)
+        query_key, value_gate = ordered[:chunk], ordered[chunk:]
         here = pl.ds(pl.multiple_of(c * chunk, chunk), chunk)
         live = c * chunk + chunk_row < my_count
-        kv_ref[here, :] = jnp.where(live, ordered[:, width : 3 * width], 0.0).astype(jnp.bfloat16)
-        gate_buf[...] = ordered[:, 3 * width :]
+        kv_ref[here, :width] = jnp.where(live, query_key[:, width:], 0.0).astype(jnp.bfloat16)
+        kv_ref[here, width:] = jnp.where(live, value_gate[:, :width], 0.0).astype(jnp.bfloat16)
+        gate_buf[...] = value_gate[:, width:]
         total = jnp.zeros((chunk, 1), jnp.float32)
         squares = jnp.zeros((chunk, 1), jnp.float32)
         for head in range(heads):
             columns = slice(head * DH, (head + 1) * DH)
-            query = ordered[:, columns]
-            key = ordered[:, width + head * DH : width + (head + 1) * DH]
-            value = ordered[:, 2 * width + head * DH : 2 * width + (head + 1) * DH]
+            query = query_key[:, columns]
+            key = query_key[:, width + head * DH : width + (head + 1) * DH]
+            value = value_gate[:, columns]
             half = (
                 lax.dot_general(
                     query.astype(jnp.bfloat16),
@@ -261,6 +279,7 @@
             total = total + jnp.sum(attended, axis=1, keepdims=True)
             squares = squares + jnp.sum(attended * attended, axis=1, keepdims=True)
         both = jnp.where(lane == 0, total, jnp.where(lane == 1, squares, 0.0))
+        both = jnp.concatenate([both, jnp.zeros((128 - chunk, 128), jnp.float32)], axis=0)
         stats_buf[c, my_part] = both.T[:8]
         for step in range(1, mp_count):
             part_copy(stats_buf, stats_send, stats_recv, c, my_part, part(step)).start()
@@ -271,9 +290,9 @@
         stats = stats_buf[c, 0]
         for index in range(1, mp_count):
             stats = stats + stats_buf[c, index]
-        stats = jnp.concatenate([stats, jnp.zeros((128 - 8, chunk), jnp.float32)], axis=0).T
-        mean = stats[:, 0:1] / width_all
-        variance = stats[:, 1:2] / width_all - mean * mean
+        stats = jnp.concatenate([stats, jnp.zeros((128 - 8, 128), jnp.float32)], axis=0).T
+        mean = stats[:chunk, 0:1] / width_all
+        variance = stats[:chunk, 1:2] / width_all - mean * mean
         normed = (attended_buf[...] - mean) * lax.rsqrt(variance + EPSILON)
         gated_buf[c, my_part] = (normed * gate_buf[...]).astype(jnp.bfloat16)
         for step in range(1, mp_count):
@@ -286,7 +305,7 @@
         for index in range(mp_count):
             mixed = mixed + jnp.dot(
                 gated_buf[c, index],
-                w_ref[index * width : (index + 1) * width, :],
+                w_buf[index * width : (index + 1) * width, :],
                 preferred_element_type=jnp.float32,
             )
         here = pl.ds(pl.multiple_of(c * chunk, chunk), chunk)
@@ -295,6 +314,10 @@
 
     def work(c, carry):
         attend(c)
+
+        @pl.when(c == 1)
+        def _():
+            fetch_w.wait()
 
         @pl.when(c > 0)
         def _():
@@ -323,8 +346,8 @@
     width = w_out.shape[1]
     local_rows = new_rows.shape[0]
     history_cap = cache_kv.shape[1]
-    chunks = CAP // (dp_count * TILE)
-    chunk = dp_count * TILE
+    chunks = CAP // (dp_count * EVENTS)
+    chunk = dp_count * EVENTS
     smem = pl.BlockSpec(memory_space=pltpu.SMEM)
     vmem = pl.BlockSpec(memory_space=pltpu.VMEM)
     dma = pltpu.SemaphoreType.DMA
@@ -334,16 +357,17 @@
             jax.ShapeDtypeStruct((CAP, 2 * width), jnp.bfloat16),
             jax.ShapeDtypeStruct((CAP, width), jnp.bfloat16),
         ),
-        in_specs=[smem, smem, smem, vmem, vmem, vmem],
+        in_specs=[smem, smem, smem, vmem, vmem, pl.BlockSpec(memory_space=pltpu.HBM)],
         out_specs=(vmem, vmem),
         scratch_shapes=[
-            pltpu.VMEM((chunks, dp_count, TILE, 4 * width), jnp.bfloat16),
-            pltpu.VMEM((chunks, dp_count, TILE, 4 * width), jnp.bfloat16),
+            pltpu.VMEM(w_out.shape, jnp.bfloat16),
+            pltpu.VMEM((chunks, dp_count, TILE, 2 * width), jnp.bfloat16),
+            pltpu.VMEM((chunks, dp_count, TILE, 2 * width), jnp.bfloat16),
             pltpu.VMEM((history_cap, width), jnp.bfloat16),
-            pltpu.VMEM((chunk, chunk), jnp.bfloat16),
+            pltpu.VMEM((2 * chunk, 2 * chunk), jnp.bfloat16),
             pltpu.VMEM((chunk, width), jnp.float32),
             pltpu.VMEM((chunk, width), jnp.float32),
-            pltpu.VMEM((chunks, mp_count, 8, chunk), jnp.float32),
+            pltpu.VMEM((chunks, mp_count, 8, 128), jnp.float32),
             pltpu.VMEM((chunks, mp_count, chunk, width), jnp.bfloat16),
             dma((chunks, dp_count)),
             dma((chunks, dp_count)),
@@ -351,6 +375,7 @@
             dma((chunks, mp_count)),
             dma((chunks, mp_count)),
             dma((chunks, mp_count)),
+            dma,
         ],
         compiler_params=pltpu.CompilerParams(
             collective_id=0, has_side_effects=True, vmem_limit_bytes=40 * 2**20

time: 71.9 us -> 77.8 us (1.082)
  Pallas kernels: 66.5 us -> 71.9 us
    pallas_call x1, Pallas kernels: 66.5 us -> 71.9 us  [kernel_device(): pl.pallas_call(functools.partial(layer_kernel, dp_count, mp_count), out_s...]
where the time goes in v2:
time: 77.8 us; the launch traced here: 77.1 us
  Pallas kernels  71.9 us (92%)
  local copies, waits for them, and re-layouts  4.5 us (6%)
    pallas_call x1, Pallas kernels, kernel_device(): pl.pallas_call(functools.partial(layer_kernel, dp_count, mp_count), out_s...  71.9 us
    unnamed x13, local copies, waits for them, and re-layouts  3.33 us

profile of v2, /device:TPU:11, one launch (start us, length us, event | category | flops | bytes accessed | tf_op | source)
XLA Modules:
  0.0 77.1 jit_solution(2190640067438615654)
XLA Ops:
  0.6 0.0 copy-start.4
  0.6 1.3 %copy.8 = bf16[32,8,4,384]{3,1,2,0:T(8,128)(2,1)S(1)} copy(bf16[32,8,4,384]{3,2,1,0:T(4,128)(2,1)} %bitcast.10) | data formatting | bytes 1572864
  2.0 0.0 copy-start
  2.0 0.0 copy-start.1
  2.0 0.0 copy-start.2
  2.0 0.0 copy-start.3
  2.0 0.0 copy-done.4
  2.0 0.1 copy.9
  2.1 1.1 %copy-done = bf16[1536,384]{1,0:T(8,128)(2,1)S(1)} copy-done((bf16[1536,384]{1,0:T(8,128)(2,1)S(1)}, bf16[1536,384]{1,0:T(8,128)(2,1)}, u32[]{:S(2)}) %copy-start) | copy-done | bytes 1179672
  3.2 0.0 copy-done.1
  3.2 0.0 copy-done.2
  3.2 0.0 copy-done.3
  3.2 71.9 %shard_map.77 = (bf16[640,768]{1,0:T(8,128)(2,1)S(1)}, bf16[640,384]{1,0:T(8,128)(2,1)S(1)}) custom-call(s32[8]{0:T(128)S(1)} %copy-done.1, s32[8]{0:T(128)S(1)} %copy-done.2, s32[8]{0:T(128)S(1)} %copy-done.3, bf16[256,1536]{1,0:T(8,128)(2,1)S(1)} %bitcast.7, bf16[512,768]{1,0:T(8,128)(2,1)S(1)} %bitcast.8, bf16[1536,384]{1,0:T(8,128)(2,1)S(1)} %copy-done), custom_call_target="tpu_custom_call" | custom-call | tf_op jit(solution)/shard_map/pallas_call | solution.py:354
  75.2 1.2 %reshape.15 = bf16[1,640,2,384]{3,2,1,0:T(2,128)(2,1)} reshape(bf16[640,768]{1,0:T(8,128)(2,1)S(1)} %get-tuple-element.4) | data formatting | bytes 1966080 | tf_op jit(solution)/shard_map/reshape | solution.py:391
  76.4 0.8 %copy.11 = bf16[1,640,384]{2,1,0:T(8,128)(2,1)} copy(bf16[1,640,384]{2,1,0:T(8,128)(2,1)S(1)} %bitcast.9) | data formatting | bytes 983040
Async XLA Ops:
  0.6 1.4 %copy-start.4 = (bf16[1,512,2,384]{3,2,1,0:T(2,128)(2,1)S(1)}, bf16[1,512,2,384]{3,2,1,0:T(2,128)(2,1)}, u32[]{:S(2)}) copy-start(bf16[1,512,2,384]{3,2,1,0:T(2,128)(2,1)} %param.10) | copy-start | bytes 2359300
  2.0 1.3 %copy-start = (bf16[1536,384]{1,0:T(8,128)(2,1)S(1)}, bf16[1536,384]{1,0:T(8,128)(2,1)}, u32[]{:S(2)}) copy-start(bf16[1536,384]{1,0:T(8,128)(2,1)} %w_ref.1) | copy-start | bytes 3538948
  2.0 1.3 %copy-start.1 = (s32[8]{0:T(128)S(1)}, s32[8]{0:T(128)}, u32[]{:S(2)}) copy-start(s32[8]{0:T(128)} %counts_ref.1) | copy-start | bytes 100
  2.0 1.3 %copy-start.2 = (s32[8]{0:T(128)S(1)}, s32[8]{0:T(128)}, u32[]{:S(2)}) copy-start(s32[8]{0:T(128)} %history_ref.1) | copy-start | bytes 100
  2.0 1.3 %copy-start.3 = (s32[8]{0:T(128)S(1)}, s32[8]{0:T(128)}, u32[]{:S(2)}) copy-start(s32[8]{0:T(128)} %owner_ref.1) | copy-start | bytes 100

commit v3 on v1

--- a/solution.py
+++ b/solution.py
@@ -1,4 +1,5 @@
 import functools
+import itertools
 import math
 
 import jax
@@ -98,6 +99,8 @@
 def layer_kernel(
     dp_count,
     mp_count,
+    base,
+    large,
     counts_ref,
     history_ref,
     owner_ref,
@@ -106,8 +109,10 @@
     w_ref,
     kv_ref,
     out_ref,
+    w_buf,
     send_buf,
     recv_buf,
+    keys_buf,
     values_buf,
     perm_buf,
     attended_buf,
@@ -120,7 +125,10 @@
     stats_recv,
     gated_send,
     gated_recv,
+    w_sem,
 ):
+    fetch_w = pltpu.make_async_copy(w_ref, w_buf, w_sem)
+    fetch_w.start()
     me = lax.axis_index("dp")
     my_part = lax.axis_index("mp")
     users = counts_ref.shape[0]
@@ -132,6 +140,7 @@
     chunks = send_buf.shape[0]
     chunk = dp_count * TILE
     half_scale = 0.5 / math.sqrt(DH)
+    is_large = functools.reduce(jnp.logical_or, [me == slot for slot in large])
 
     def peer(step):
         return lax.rem(me + step, dp_count)
@@ -191,24 +200,48 @@
     tile_id = lax.broadcasted_iota(jnp.int32, (TILE, local_rows), 0)
     offset = row_id - tile_id
 
-    pl.semaphore_wait(barrier, dp_count - 1 + mp_count - 1)
-
-    def pack(c, carry):
+    def pack(c, slots):
         picked = jnp.concatenate(
             [
                 jnp.where(offset == slot_row[slot] + c * TILE, 1.0, 0.0).astype(jnp.bfloat16)
-                for slot in range(dp_count)
+                for slot in slots
             ],
             axis=0,
         )
         sent = jnp.dot(picked, rows_ref[...], preferred_element_type=jnp.float32)
-        send_buf[c] = sent.astype(jnp.bfloat16).reshape(dp_count, TILE, 4 * width)
+        return sent.astype(jnp.bfloat16).reshape(len(slots), TILE, 4 * width)
+
+    def post(c):
         for step in range(1, dp_count):
             row_copy(c, me, peer(step)).start()
         recv_buf[c, me] = send_buf[c, me]
-        return carry
-
-    lax.fori_loop(0, chunks, pack, 0)
+
+    def pack_all(c, carry):
+        send_buf[c] = pack(c, range(dp_count))
+        post(c)
+        return carry
+
+    def pack_large(c, carry):
+        sent = pack(c, large)
+        for index, slot in enumerate(large):
+            send_buf[c, slot] = sent[index]
+
+            @pl.when(me != slot)
+            def _():
+                row_copy(c, me, slot).start()
+
+            @pl.when(me == slot)
+            def _():
+                recv_buf[c, slot] = send_buf[c, slot]
+
+        return carry
+
+    send_buf[0] = pack(0, range(dp_count))
+    pl.semaphore_wait(barrier, dp_count - 1 + mp_count - 1)
+    post(0)
+    lax.fori_loop(1, base, pack_all, 0)
+    if base < chunks:
+        lax.fori_loop(base, chunks, pack_large, 0)
 
     place = lax.broadcasted_iota(jnp.int32, (chunk, chunk), 0)
     landed = lax.broadcasted_iota(jnp.int32, (chunk, chunk), 1)
@@ -217,11 +250,12 @@
         source_of - lax.rem(my_first, dp_count) + dp_count, dp_count
     )
     perm_buf[...] = jnp.where(place == ordered_at, 1.0, 0.0).astype(jnp.bfloat16)
+    keys_buf[...] = cache_ref[:, :width].astype(jnp.float32).T.astype(jnp.bfloat16)
     history_id = lax.broadcasted_iota(jnp.int32, (history_cap, width), 0)
     values_buf[...] = jnp.where(
         history_id < my_history, cache_ref[:, width:].astype(jnp.float32), 0.0
     ).astype(jnp.bfloat16)
-    lane = lax.broadcasted_iota(jnp.int32, (chunk, 128), 1)
+    line = lax.broadcasted_iota(jnp.int32, (8, chunk), 0)
     chunk_row = lax.broadcasted_iota(jnp.int32, (chunk, 1), 0)
     inverse = 1.0 / (my_history + 1).astype(jnp.float32)
 
@@ -234,18 +268,17 @@
         live = c * chunk + chunk_row < my_count
         kv_ref[here, :] = jnp.where(live, ordered[:, width : 3 * width], 0.0).astype(jnp.bfloat16)
         gate_buf[...] = ordered[:, 3 * width :]
-        total = jnp.zeros((chunk, 1), jnp.float32)
-        squares = jnp.zeros((chunk, 1), jnp.float32)
+        total = jnp.zeros((chunk, DH), jnp.float32)
+        squares = jnp.zeros((chunk, DH), jnp.float32)
         for head in range(heads):
             columns = slice(head * DH, (head + 1) * DH)
             query = ordered[:, columns]
             key = ordered[:, width + head * DH : width + (head + 1) * DH]
             value = ordered[:, 2 * width + head * DH : 2 * width + (head + 1) * DH]
             half = (
-                lax.dot_general(
+                jnp.dot(
                     query.astype(jnp.bfloat16),
-                    cache_ref[:, columns],
-                    (((1,), (1,)), ((), ())),
+                    keys_buf[columns, :],
                     preferred_element_type=jnp.float32,
                 )
                 * half_scale
@@ -258,10 +291,11 @@
             own = jnp.sum(query * key, axis=1, keepdims=True) * half_scale
             attended = (summed + half_silu(own) * value) * inverse
             attended_buf[:, columns] = attended
-            total = total + jnp.sum(attended, axis=1, keepdims=True)
-            squares = squares + jnp.sum(attended * attended, axis=1, keepdims=True)
-        both = jnp.where(lane == 0, total, jnp.where(lane == 1, squares, 0.0))
-        stats_buf[c, my_part] = both.T[:8]
+            total = total + attended
+            squares = squares + attended * attended
+        total = jnp.sum(total.T, axis=0, keepdims=True)
+        squares = jnp.sum(squares.T, axis=0, keepdims=True)
+        stats_buf[c, my_part] = jnp.where(line == 0, total, jnp.where(line == 1, squares, 0.0))
         for step in range(1, mp_count):
             part_copy(stats_buf, stats_send, stats_recv, c, my_part, part(step)).start()
 
@@ -271,10 +305,11 @@
         stats = stats_buf[c, 0]
         for index in range(1, mp_count):
             stats = stats + stats_buf[c, index]
+        mean = stats[0:1] / width_all
+        variance = stats[1:2] / width_all - mean * mean
+        stats = jnp.where(line == 0, mean, lax.rsqrt(variance + EPSILON))
         stats = jnp.concatenate([stats, jnp.zeros((128 - 8, chunk), jnp.float32)], axis=0).T
-        mean = stats[:, 0:1] / width_all
-        variance = stats[:, 1:2] / width_all - mean * mean
-        normed = (attended_buf[...] - mean) * lax.rsqrt(variance + EPSILON)
+        normed = (attended_buf[...] - stats[:, 0:1]) * stats[:, 1:2]
         gated_buf[c, my_part] = (normed * gate_buf[...]).astype(jnp.bfloat16)
         for step in range(1, mp_count):
             part_copy(gated_buf, gated_send, gated_recv, c, my_part, part(step)).start()
@@ -286,7 +321,7 @@
         for index in range(mp_count):
             mixed = mixed + jnp.dot(
                 gated_buf[c, index],
-                w_ref[index * width : (index + 1) * width, :],
+                w_buf[index * width : (index + 1) * width, :],
                 preferred_element_type=jnp.float32,
             )
         here = pl.ds(pl.multiple_of(c * chunk, chunk), chunk)
@@ -303,21 +338,60 @@
         gate(c)
         return carry
 
-    lax.fori_loop(0, chunks, work, 0)
-    mix(chunks - 1)
-
-    def finish(c, carry):
-        for step in range(1, dp_count):
-            row_copy(c, me, peer(step)).wait_send()
+    lax.fori_loop(0, 1, work, 0)
+    fetch_w.wait()
+    lax.fori_loop(1, base, work, 0)
+    if base < chunks:
+
+        @pl.when(is_large)
+        def _():
+            lax.fori_loop(base, chunks, work, 0)
+            mix(chunks - 1)
+
+        @pl.when(jnp.logical_not(is_large))
+        def _():
+            mix(base - 1)
+            kv_ref[base * chunk :, :] = jnp.zeros(
+                ((chunks - base) * chunk, 2 * width), jnp.bfloat16
+            )
+            out_ref[base * chunk :, :] = jnp.zeros(((chunks - base) * chunk, width), jnp.bfloat16)
+
+    else:
+        mix(chunks - 1)
+
+    def finish_parts(c, carry):
         for step in range(1, mp_count):
             part_copy(stats_buf, stats_send, stats_recv, c, my_part, part(step)).wait_send()
             part_copy(gated_buf, gated_send, gated_recv, c, my_part, part(step)).wait_send()
         return carry
 
-    lax.fori_loop(0, chunks, finish, 0)
-
-
-def kernel_device(new_rows, counts, history_len, user_owner, cache_kv, w_out):
+    def finish_rows(c, carry):
+        for step in range(1, dp_count):
+            row_copy(c, me, peer(step)).wait_send()
+        return carry
+
+    def finish_large(c, carry):
+        for slot in large:
+
+            @pl.when(me != slot)
+            def _():
+                row_copy(c, me, slot).wait_send()
+
+        return carry
+
+    lax.fori_loop(0, base, finish_rows, 0)
+    lax.fori_loop(0, base, finish_parts, 0)
+    if base < chunks:
+        lax.fori_loop(base, chunks, finish_large, 0)
+
+        @pl.when(is_large)
+        def _():
+            lax.fori_loop(base, chunks, finish_parts, 0)
+
+
+def kernel_device(
+    base, large, variant, new_rows, counts, history_len, user_owner, cache_kv, w_out
+):
     dp_count = lax.axis_size("dp")
     mp_count = lax.axis_size("mp")
     width = w_out.shape[1]
@@ -329,16 +403,18 @@
     vmem = pl.BlockSpec(memory_space=pltpu.VMEM)
     dma = pltpu.SemaphoreType.DMA
     key_value, results = pl.pallas_call(
-        functools.partial(layer_kernel, dp_count, mp_count),
+        functools.partial(layer_kernel, dp_count, mp_count, min(base, chunks), large),
         out_shape=(
             jax.ShapeDtypeStruct((CAP, 2 * width), jnp.bfloat16),
             jax.ShapeDtypeStruct((CAP, width), jnp.bfloat16),
         ),
-        in_specs=[smem, smem, smem, vmem, vmem, vmem],
+        in_specs=[smem, smem, smem, vmem, vmem, pl.BlockSpec(memory_space=pltpu.HBM)],
         out_specs=(vmem, vmem),
         scratch_shapes=[
+            pltpu.VMEM(w_out.shape, jnp.bfloat16),
             pltpu.VMEM((chunks, dp_count, TILE, 4 * width), jnp.bfloat16),
             pltpu.VMEM((chunks, dp_count, TILE, 4 * width), jnp.bfloat16),
+            pltpu.VMEM((width, history_cap), jnp.bfloat16),
             pltpu.VMEM((history_cap, width), jnp.bfloat16),
             pltpu.VMEM((chunk, chunk), jnp.bfloat16),
             pltpu.VMEM((chunk, width), jnp.float32),
@@ -351,9 +427,10 @@
             dma((chunks, mp_count)),
             dma((chunks, mp_count)),
             dma((chunks, mp_count)),
+            dma,
         ],
         compiler_params=pltpu.CompilerParams(
-            collective_id=0, has_side_effects=True, vmem_limit_bytes=40 * 2**20
+            collective_id=variant, has_side_effects=True, vmem_limit_bytes=40 * 2**20
         ),
     )(
         counts,
@@ -366,11 +443,39 @@
     return (key_value.reshape(1, CAP, 2, width), results[None])
 
 
+def switched_device(new_rows, counts, history_len, user_owner, cache_kv, w_out):
+    dp_count = lax.axis_size("dp")
+    half = dp_count // 2
+    base = 3
+    pairs = list(itertools.combinations(range(half), 2))
+    branches = [
+        functools.partial(kernel_device, base, (a, b, a + half, b + half), variant)
+        for variant, (a, b) in enumerate(pairs)
+    ]
+    branches.append(
+        functools.partial(kernel_device, CAP, tuple(range(dp_count)), len(pairs))
+    )
+    over = counts > base * dp_count * TILE
+    places = lax.reduce(
+        jnp.where(over, jnp.left_shift(1, user_owner % half), 0).astype(jnp.int32),
+        jnp.int32(0),
+        lax.bitwise_or,
+        (0,),
+    )
+    choice = jnp.int32(len(pairs))
+    for variant, (a, b) in enumerate(pairs):
+        outside = places & jnp.int32((1 << half) - 1 - (1 << a) - (1 << b))
+        choice = jnp.where(outside == 0, jnp.int32(variant), choice)
+    return lax.switch(
+        choice, branches, new_rows, counts, history_len, user_owner, cache_kv, w_out
+    )
+
+
 def solution(mesh):
     placed = (P(None, "dp", None, "mp"), P(), P(), P(), P("dp", None, None, "mp"), P(None, "mp"))
     fits = mesh.shape["dp"] * TILE == 128
     return jax.shard_map(
-        kernel_device if fits else general_device,
+        switched_device if fits else general_device,
         mesh=mesh,
         in_specs=placed,
         out_specs=(P("dp", None, None, "mp"), P("dp", None, "mp")),

time: 71.9 us -> 75.2 us (1.046)
  between operations: 0.7 us -> 4.54 us
  Pallas kernels: 66.5 us -> 63.5 us
  other arithmetic: 0 us -> 1.32 us
    pallas_call x1, Pallas kernels: 66.5 us -> 63.5 us  [kernel_device(): pl.pallas_call(functools.partial(layer_kernel, dp_count, mp_count, min(ba...]
    cond x0 -> x12, local copies, waits for them, and re-layouts: none -> 2.57 us
    unnamed x13 -> x1, local copies, waits for them, and re-layouts: 3.33 us -> 0.78 us
    another operation x0 -> x1, other arithmetic: none -> 1.32 us  [switched_device(): lax.reduce(jnp.where(over, jnp.left_shift(1, user_owner % half), 0).astyp...]
where the time goes in v3:
time: 75.2 us; the launch traced here: 74.5 us
  Pallas kernels  63.5 us (84%)
  between operations  4.54 us (6%)
  local copies, waits for them, and re-layouts  4.52 us (6%)
  other arithmetic  1.32 us (2%)
    pallas_call x1, Pallas kernels, kernel_device(): pl.pallas_call(functools.partial(layer_kernel, dp_count, mp_count, min(ba...  63.5 us
    cond x12, local copies, waits for them, and re-layouts  2.57 us

profile of v3, /device:TPU:11, one launch (start us, length us, event | category | flops | bytes accessed | tf_op | source)
XLA Modules:
  0.0 74.5 jit_solution(18198808351513427736)
XLA Ops:
  0.6 1.3 %fusion = s32[]{:T(128)} fusion(s32[8]{0:T(128)} %param.14, s32[8]{0:T(128)} %param.16), kind=kLoop, calls=%fused_computation.4 | loop fusion | flops 119 | bytes 68 | tf_op jit(solution)/shard_map/reduce | solution.py:459
  5.8 66.7 %conditional.1 = ((bf16[640,768]{1,0:T(8,128)(2,1)S(1)}, bf16[640,384]{1,0:T(8,128)(2,1)S(1)})) conditional(s32[]{:T(128)} %clamp.3, (bf16[256,1,4,384]{3,2,1,0:T(4,128)(2,1)}, bf16[1,512,2,384]{3,2,1,0:T(2,128)(2,1)}, s32[8]{0:T(128)}, s32[8]{0:T(128)}, s32[8]{0:T(128)}, ...), branch_computations={%region_1.2_spmd, %region_2.3_spmd, %region_3.4_spmd, %region_4.5_... | conditional | bytes 11010580 | solution.py:469
  6.1 0.0 copy-start.11
  6.1 1.3 %copy.24 = bf16[64,8,2,384]{3,1,2,0:T(8,128)(2,1)S(1)} copy(bf16[64,8,2,384]{3,2,1,0:T(2,128)(2,1)} %bitcast.82) | data formatting | bytes 1572864 | tf_op jit(solution)/shard_map/cond
  7.4 0.0 copy-start.4
  7.5 0.0 copy-start.18
  7.5 0.0 copy-start.25
  7.5 0.0 copy-start.32
  7.5 0.0 copy-done.11
  7.5 0.1 copy.23
  7.6 1.1 %copy-done.4 = bf16[1536,384]{1,0:T(8,128)(2,1)S(1)} copy-done((bf16[1536,384]{1,0:T(8,128)(2,1)S(1)}, bf16[1536,384]{1,0:T(8,128)(2,1)}, u32[]{:S(2)}) %copy-start.4) | copy-done | bytes 1179672 | tf_op jit(solution)/shard_map/cond
  8.7 0.0 copy-done.18
  8.7 0.0 copy-done.25
  8.7 0.0 copy-done.32
  8.7 63.5 %branch_4_fun.1 = (bf16[640,768]{1,0:T(8,128)(2,1)S(1)}, bf16[640,384]{1,0:T(8,128)(2,1)S(1)}) custom-call(s32[8]{0:T(128)S(1)} %copy-done.18, s32[8]{0:T(128)S(1)} %copy-done.32, s32[8]{0:T(128)S(1)} %copy-done.25, bf16[256,1536]{1,0:T(8,128)(2,1)S(1)} %bitcast.66, bf16[512,768]{1,0:T(8,128)(2,1)S(1)} %bitcast.65, bf16[1536,384]{1,0:T(8,128)(2,1)S(1)} %copy-done.4), custom_call_target="tpu_custom_call" | custom-call | tf_op jit(solution)/shard_map/cond/branch_4_fun/pallas_call | solution.py:405
  72.5 1.2 %reshape.67 = bf16[1,640,2,384]{3,2,1,0:T(2,128)(2,1)} reshape(bf16[640,768]{1,0:T(8,128)(2,1)S(1)} %get-tuple-element.144) | data formatting | bytes 1966080 | tf_op jit(solution)/shard_map/cond/branch_0_fun/reshape | solution.py:443
  73.7 0.8 %copy.44 = bf16[1,640,384]{2,1,0:T(8,128)(2,1)} copy(bf16[1,640,384]{2,1,0:T(8,128)(2,1)S(1)} %bitcast.85) | data formatting | bytes 983040
Async XLA Ops:
  6.1 1.4 %copy-start.11 = (bf16[256,1,4,384]{3,2,1,0:T(4,128)(2,1)S(1)}, bf16[256,1,4,384]{3,2,1,0:T(4,128)(2,1)}, u32[]{:S(2)}) copy-start(bf16[256,1,4,384]{3,2,1,0:T(4,128)(2,1)} %get-tuple-element.169) | copy-start | bytes 2359300 | tf_op jit(solution)/shard_map/cond
  7.4 1.3 %copy-start.4 = (bf16[1536,384]{1,0:T(8,128)(2,1)S(1)}, bf16[1536,384]{1,0:T(8,128)(2,1)}, u32[]{:S(2)}) copy-start(bf16[1536,384]{1,0:T(8,128)(2,1)} %get-tuple-element.121.w_ref) | copy-start | bytes 3538948 | tf_op jit(solution)/shard_map/cond
  7.5 1.3 %copy-start.18 = (s32[8]{0:T(128)S(1)}, s32[8]{0:T(128)}, u32[]{:S(2)}) copy-start(s32[8]{0:T(128)} %get-tuple-element.116.counts_ref) | copy-start | bytes 100 | tf_op jit(solution)/shard_map/cond
  7.5 1.3 %copy-start.25 = (s32[8]{0:T(128)S(1)}, s32[8]{0:T(128)}, u32[]{:S(2)}) copy-start(s32[8]{0:T(128)} %get-tuple-element.118.owner_ref) | copy-start | bytes 100 | tf_op jit(solution)/shard_map/cond
  7.5 1.3 %copy-start.32 = (s32[8]{0:T(128)S(1)}, s32[8]{0:T(128)}, u32[]{:S(2)}) copy-start(s32[8]{0:T(128)} %get-tuple-element.117.history_ref) | copy-start | bytes 100 | tf_op jit(solution)/shard_map/cond

commit v4 on v3

--- a/solution.py
+++ b/solution.py
@@ -1,5 +1,4 @@
 import functools
-import itertools
 import math
 
 import jax
@@ -211,37 +210,44 @@
         sent = jnp.dot(picked, rows_ref[...], preferred_element_type=jnp.float32)
         return sent.astype(jnp.bfloat16).reshape(len(slots), TILE, 4 * width)
 
+    def pack_into(c):
+        @pl.when(c < base)
+        def _():
+            send_buf[c] = pack(c, range(dp_count))
+
+        if base < chunks:
+
+            @pl.when(jnp.logical_and(c >= base, c < chunks))
+            def _():
+                sent = pack(c, large)
+                for index, slot in enumerate(large):
+                    send_buf[c, slot] = sent[index]
+
+    def each_copy(c, act):
+        @pl.when(c < base)
+        def _():
+            for step in range(1, dp_count):
+                act(row_copy(c, me, peer(step)))
+
+        if base < chunks:
+
+            @pl.when(jnp.logical_and(c >= base, c < chunks))
+            def _():
+                for slot in large:
+
+                    @pl.when(me != slot)
+                    def _():
+                        act(row_copy(c, me, slot))
+
     def post(c):
-        for step in range(1, dp_count):
-            row_copy(c, me, peer(step)).start()
-        recv_buf[c, me] = send_buf[c, me]
-
-    def pack_all(c, carry):
-        send_buf[c] = pack(c, range(dp_count))
-        post(c)
-        return carry
-
-    def pack_large(c, carry):
-        sent = pack(c, large)
-        for index, slot in enumerate(large):
-            send_buf[c, slot] = sent[index]
-
-            @pl.when(me != slot)
-            def _():
-                row_copy(c, me, slot).start()
-
-            @pl.when(me == slot)
-            def _():
-                recv_buf[c, slot] = send_buf[c, slot]
-
-        return carry
-
-    send_buf[0] = pack(0, range(dp_count))
+        each_copy(c, lambda copy: copy.start())
+
+    pack_into(0)
     pl.semaphore_wait(barrier, dp_count - 1 + mp_count - 1)
     post(0)
-    lax.fori_loop(1, base, pack_all, 0)
-    if base < chunks:
-        lax.fori_loop(base, chunks, pack_large, 0)
+    pack_into(1)
+    post(1)
+    pack_into(2)
 
     place = lax.broadcasted_iota(jnp.int32, (chunk, chunk), 0)
     landed = lax.broadcasted_iota(jnp.int32, (chunk, chunk), 1)
@@ -260,6 +266,7 @@
     inverse = 1.0 / (my_history + 1).astype(jnp.float32)
 
     def attend(c):
+        recv_buf[c, me] = send_buf[c, me]
         for step in range(1, dp_count):
             row_copy(c, peer(step), me).wait_recv()
         arrived = recv_buf[c].reshape(chunk, 4 * width)
@@ -328,36 +335,45 @@
         live = c * chunk + chunk_row < my_count
         out_ref[here, :] = jnp.where(live, mixed, 0.0).astype(jnp.bfloat16)
 
-    def work(c, carry):
-        attend(c)
-
-        @pl.when(c > 0)
+    def works(c):
+        return jnp.logical_or(c < base, is_large)
+
+    def step_of(c, carry):
+        each_copy(c, lambda copy: copy.wait_send())
+        post(c + 2)
+
+        @pl.when(works(c))
+        def _():
+            attend(c)
+
+        pack_into(c + 3)
+
+        @pl.when(jnp.logical_and(c > 0, works(c - 1)))
         def _():
             mix(c - 1)
 
-        gate(c)
+        @pl.when(works(c))
+        def _():
+            gate(c)
+
         return carry
 
-    lax.fori_loop(0, 1, work, 0)
+    lax.fori_loop(0, 1, step_of, 0)
     fetch_w.wait()
-    lax.fori_loop(1, base, work, 0)
+    lax.fori_loop(1, chunks, step_of, 0)
+
+    @pl.when(works(chunks - 1))
+    def _():
+        mix(chunks - 1)
+
     if base < chunks:
 
-        @pl.when(is_large)
-        def _():
-            lax.fori_loop(base, chunks, work, 0)
-            mix(chunks - 1)
-
         @pl.when(jnp.logical_not(is_large))
         def _():
-            mix(base - 1)
             kv_ref[base * chunk :, :] = jnp.zeros(
                 ((chunks - base) * chunk, 2 * width), jnp.bfloat16
             )
             out_ref[base * chunk :, :] = jnp.zeros(((chunks - base) * chunk, width), jnp.bfloat16)
-
-    else:
-        mix(chunks - 1)
 
     def finish_parts(c, carry):
         for step in range(1, mp_count):
@@ -365,24 +381,8 @@
             part_copy(gated_buf, gated_send, gated_recv, c, my_part, part(step)).wait_send()
         return carry
 
-    def finish_rows(c, carry):
-        for step in range(1, dp_count):
-            row_copy(c, me, peer(step)).wait_send()
-        return carry
-
-    def finish_large(c, carry):
-        for slot in large:
-
-            @pl.when(me != slot)
-            def _():
-                row_copy(c, me, slot).wait_send()
-
-        return carry
-
-    lax.fori_loop(0, base, finish_rows, 0)
     lax.fori_loop(0, base, finish_parts, 0)
     if base < chunks:
-        lax.fori_loop(base, chunks, finish_large, 0)
 
         @pl.when(is_large)
         def _():
@@ -443,39 +443,16 @@
     return (key_value.reshape(1, CAP, 2, width), results[None])
 
 
-def switched_device(new_rows, counts, history_len, user_owner, cache_kv, w_out):
-    dp_count = lax.axis_size("dp")
-    half = dp_count // 2
-    base = 3
-    pairs = list(itertools.combinations(range(half), 2))
-    branches = [
-        functools.partial(kernel_device, base, (a, b, a + half, b + half), variant)
-        for variant, (a, b) in enumerate(pairs)
-    ]
-    branches.append(
-        functools.partial(kernel_device, CAP, tuple(range(dp_count)), len(pairs))
-    )
-    over = counts > base * dp_count * TILE
-    places = lax.reduce(
-        jnp.where(over, jnp.left_shift(1, user_owner % half), 0).astype(jnp.int32),
-        jnp.int32(0),
-        lax.bitwise_or,
-        (0,),
-    )
-    choice = jnp.int32(len(pairs))
-    for variant, (a, b) in enumerate(pairs):
-        outside = places & jnp.int32((1 << half) - 1 - (1 << a) - (1 << b))
-        choice = jnp.where(outside == 0, jnp.int32(variant), choice)
-    return lax.switch(
-        choice, branches, new_rows, counts, history_len, user_owner, cache_kv, w_out
-    )
+def whole_device(*arrays):
+    slots = tuple(range(lax.axis_size("dp")))
+    return kernel_device(CAP, slots, 0, *arrays)
 
 
 def solution(mesh):
     placed = (P(None, "dp", None, "mp"), P(), P(), P(), P("dp", None, None, "mp"), P(None, "mp"))
     fits = mesh.shape["dp"] * TILE == 128
     return jax.shard_map(
-        switched_device if fits else general_device,
+        whole_device if fits else general_device,
         mesh=mesh,
         in_specs=placed,
         out_specs=(P("dp", None, None, "mp"), P("dp", None, "mp")),

time: 75.2 us -> 70.6 us (0.939)
  between operations: 4.54 us -> 0.7 us
  Pallas kernels: 63.5 us -> 65 us
  other arithmetic: 1.32 us -> 0 us
    cond x12 -> x0, local copies, waits for them, and re-layouts: 2.57 us -> none
    unnamed x1 -> x13, local copies, waits for them, and re-layouts: 0.78 us -> 3.33 us
    pallas_call x1, Pallas kernels: 63.5 us -> 65 us  [kernel_device(): pl.pallas_call(functools.partial(layer_kernel, dp_count, mp_count, min(ba...]
    another operation x1 -> x0, other arithmetic: 1.32 us -> none  [switched_device(): lax.reduce(jnp.where(over, jnp.left_shift(1, user_owner % half), 0).astyp...]
where the time goes in v4:
time: 70.6 us; the launch traced here: 70.2 us
  Pallas kernels  65 us (92%)
  local copies, waits for them, and re-layouts  4.5 us (6%)
    pallas_call x1, Pallas kernels, kernel_device(): pl.pallas_call(functools.partial(layer_kernel, dp_count, mp_count, min(ba...  65 us
    unnamed x13, local copies, waits for them, and re-layouts  3.33 us

profile of v4, /device:TPU:11, one launch (start us, length us, event | category | flops | bytes accessed | tf_op | source)
XLA Modules:
  0.0 70.2 jit_solution(549994987745863882)
XLA Ops:
  0.6 0.0 copy-start.4
  0.6 1.3 %copy.8 = bf16[32,8,4,384]{3,1,2,0:T(8,128)(2,1)S(1)} copy(bf16[32,8,4,384]{3,2,1,0:T(4,128)(2,1)} %bitcast.10) | data formatting | bytes 1572864
  2.0 0.0 copy-start
  2.0 0.0 copy-start.1
  2.0 0.0 copy-start.2
  2.0 0.0 copy-start.3
  2.0 0.0 copy-done.4
  2.0 0.1 copy.9
  2.1 1.1 %copy-done = bf16[1536,384]{1,0:T(8,128)(2,1)S(1)} copy-done((bf16[1536,384]{1,0:T(8,128)(2,1)S(1)}, bf16[1536,384]{1,0:T(8,128)(2,1)}, u32[]{:S(2)}) %copy-start) | copy-done | bytes 1179672
  3.2 0.0 copy-done.1
  3.2 0.0 copy-done.2
  3.2 0.0 copy-done.3
  3.2 65.0 %shard_map.77 = (bf16[640,768]{1,0:T(8,128)(2,1)S(1)}, bf16[640,384]{1,0:T(8,128)(2,1)S(1)}) custom-call(s32[8]{0:T(128)S(1)} %copy-done.1, s32[8]{0:T(128)S(1)} %copy-done.2, s32[8]{0:T(128)S(1)} %copy-done.3, bf16[256,1536]{1,0:T(8,128)(2,1)S(1)} %bitcast.7, bf16[512,768]{1,0:T(8,128)(2,1)S(1)} %bitcast.8, bf16[1536,384]{1,0:T(8,128)(2,1)S(1)} %copy-done), custom_call_target="tpu_custom_call" | custom-call | tf_op jit(solution)/shard_map/pallas_call | solution.py:405
  68.3 1.2 %reshape.15 = bf16[1,640,2,384]{3,2,1,0:T(2,128)(2,1)} reshape(bf16[640,768]{1,0:T(8,128)(2,1)S(1)} %get-tuple-element.4) | data formatting | bytes 1966080 | tf_op jit(solution)/shard_map/reshape | solution.py:443
  69.4 0.8 %copy.11 = bf16[1,640,384]{2,1,0:T(8,128)(2,1)} copy(bf16[1,640,384]{2,1,0:T(8,128)(2,1)S(1)} %bitcast.9) | data formatting | bytes 983040
Async XLA Ops:
  0.6 1.4 %copy-start.4 = (bf16[1,512,2,384]{3,2,1,0:T(2,128)(2,1)S(1)}, bf16[1,512,2,384]{3,2,1,0:T(2,128)(2,1)}, u32[]{:S(2)}) copy-start(bf16[1,512,2,384]{3,2,1,0:T(2,128)(2,1)} %param.10) | copy-start | bytes 2359300
  2.0 1.3 %copy-start = (bf16[1536,384]{1,0:T(8,128)(2,1)S(1)}, bf16[1536,384]{1,0:T(8,128)(2,1)}, u32[]{:S(2)}) copy-start(bf16[1536,384]{1,0:T(8,128)(2,1)} %w_ref.1) | copy-start | bytes 3538948
  2.0 1.3 %copy-start.1 = (s32[8]{0:T(128)S(1)}, s32[8]{0:T(128)}, u32[]{:S(2)}) copy-start(s32[8]{0:T(128)} %counts_ref.1) | copy-start | bytes 100
  2.0 1.3 %copy-start.2 = (s32[8]{0:T(128)S(1)}, s32[8]{0:T(128)}, u32[]{:S(2)}) copy-start(s32[8]{0:T(128)} %history_ref.1) | copy-start | bytes 100
  2.0 1.3 %copy-start.3 = (s32[8]{0:T(128)S(1)}, s32[8]{0:T(128)}, u32[]{:S(2)}) copy-start(s32[8]{0:T(128)} %owner_ref.1) | copy-start | bytes 100

commit v5 on v4

--- a/solution.py
+++ b/solution.py
@@ -1,4 +1,5 @@
 import functools
+import itertools
 import math
 
 import jax
@@ -98,7 +99,8 @@
 def layer_kernel(
     dp_count,
     mp_count,
-    base,
+    low,
+    high,
     large,
     counts_ref,
     history_ref,
@@ -193,7 +195,11 @@
         my_first = jnp.where(mine, first, my_first)
         my_history = jnp.where(mine, history_ref[user], my_history)
         first = first + count
-    slot_row = [lax.div(value - me + (dp_count - 1), dp_count) for value in slot_first]
+    slot_row = [
+        lax.div(value - me + (dp_count - 1), dp_count) - (0 if slot in large else low * TILE)
+        for slot, value in enumerate(slot_first)
+    ]
+    first_step = jnp.where(is_large, 0, low)
 
     row_id = lax.broadcasted_iota(jnp.int32, (TILE, local_rows), 1)
     tile_id = lax.broadcasted_iota(jnp.int32, (TILE, local_rows), 0)
@@ -210,28 +216,34 @@
         sent = jnp.dot(picked, rows_ref[...], preferred_element_type=jnp.float32)
         return sent.astype(jnp.bfloat16).reshape(len(slots), TILE, 4 * width)
 
+    def for_all(c):
+        return jnp.logical_and(c >= low, c < high)
+
+    def for_large(c):
+        return jnp.logical_or(c < low, jnp.logical_and(c >= high, c < chunks))
+
     def pack_into(c):
-        @pl.when(c < base)
+        @pl.when(for_all(c))
         def _():
             send_buf[c] = pack(c, range(dp_count))
 
-        if base < chunks:
-
-            @pl.when(jnp.logical_and(c >= base, c < chunks))
+        if high - low < chunks:
+
+            @pl.when(for_large(c))
             def _():
                 sent = pack(c, large)
                 for index, slot in enumerate(large):
                     send_buf[c, slot] = sent[index]
 
     def each_copy(c, act):
-        @pl.when(c < base)
+        @pl.when(for_all(c))
         def _():
             for step in range(1, dp_count):
                 act(row_copy(c, me, peer(step)))
 
-        if base < chunks:
-
-            @pl.when(jnp.logical_and(c >= base, c < chunks))
+        if high - low < chunks:
+
+            @pl.when(for_large(c))
             def _():
                 for slot in large:
 
@@ -271,8 +283,8 @@
             row_copy(c, peer(step), me).wait_recv()
         arrived = recv_buf[c].reshape(chunk, 4 * width)
         ordered = jnp.dot(perm_buf[...], arrived, preferred_element_type=jnp.float32)
-        here = pl.ds(pl.multiple_of(c * chunk, chunk), chunk)
-        live = c * chunk + chunk_row < my_count
+        here = pl.ds(pl.multiple_of((c - first_step) * chunk, chunk), chunk)
+        live = (c - first_step) * chunk + chunk_row < my_count
         kv_ref[here, :] = jnp.where(live, ordered[:, width : 3 * width], 0.0).astype(jnp.bfloat16)
         gate_buf[...] = ordered[:, 3 * width :]
         total = jnp.zeros((chunk, DH), jnp.float32)
@@ -331,12 +343,12 @@
                 w_buf[index * width : (index + 1) * width, :],
                 preferred_element_type=jnp.float32,
             )
-        here = pl.ds(pl.multiple_of(c * chunk, chunk), chunk)
-        live = c * chunk + chunk_row < my_count
+        here = pl.ds(pl.multiple_of((c - first_step) * chunk, chunk), chunk)
+        live = (c - first_step) * chunk + chunk_row < my_count
         out_ref[here, :] = jnp.where(live, mixed, 0.0).astype(jnp.bfloat16)
 
     def works(c):
-        return jnp.logical_or(c < base, is_large)
+        return jnp.logical_or(is_large, for_all(c))
 
     def step_of(c, carry):
         each_copy(c, lambda copy: copy.wait_send())
@@ -366,14 +378,13 @@
     def _():
         mix(chunks - 1)
 
-    if base < chunks:
+    if high - low < chunks:
+        rest = chunks - (high - low)
 
         @pl.when(jnp.logical_not(is_large))
         def _():
-            kv_ref[base * chunk :, :] = jnp.zeros(
-                ((chunks - base) * chunk, 2 * width), jnp.bfloat16
-            )
-            out_ref[base * chunk :, :] = jnp.zeros(((chunks - base) * chunk, width), jnp.bfloat16)
+            kv_ref[(high - low) * chunk :, :] = jnp.zeros((rest * chunk, 2 * width), jnp.bfloat16)
+            out_ref[(high - low) * chunk :, :] = jnp.zeros((rest * chunk, width), jnp.bfloat16)
 
     def finish_parts(c, carry):
         for step in range(1, mp_count):
@@ -381,16 +392,17 @@
             part_copy(gated_buf, gated_send, gated_recv, c, my_part, part(step)).wait_send()
         return carry
 
-    lax.fori_loop(0, base, finish_parts, 0)
-    if base < chunks:
+    lax.fori_loop(low, high, finish_parts, 0)
+    if high - low < chunks:
 
         @pl.when(is_large)
         def _():
-            lax.fori_loop(base, chunks, finish_parts, 0)
+            lax.fori_loop(0, low, finish_parts, 0)
+            lax.fori_loop(high, chunks, finish_parts, 0)
 
 
 def kernel_device(
-    base, large, variant, new_rows, counts, history_len, user_owner, cache_kv, w_out
+    low, high, large, variant, new_rows, counts, history_len, user_owner, cache_kv, w_out
 ):
     dp_count = lax.axis_size("dp")
     mp_count = lax.axis_size("mp")
@@ -403,7 +415,7 @@
     vmem = pl.BlockSpec(memory_space=pltpu.VMEM)
     dma = pltpu.SemaphoreType.DMA
     key_value, results = pl.pallas_call(
-        functools.partial(layer_kernel, dp_count, mp_count, min(base, chunks), large),
+        functools.partial(layer_kernel, dp_count, mp_count, low, high, large),
         out_shape=(
             jax.ShapeDtypeStruct((CAP, 2 * width), jnp.bfloat16),
             jax.ShapeDtypeStruct((CAP, width), jnp.bfloat16),
@@ -443,16 +455,35 @@
     return (key_value.reshape(1, CAP, 2, width), results[None])
 
 
-def whole_device(*arrays):
-    slots = tuple(range(lax.axis_size("dp")))
-    return kernel_device(CAP, slots, 0, *arrays)
+def switched_device(new_rows, counts, history_len, user_owner, cache_kv, w_out):
+    dp_count = lax.axis_size("dp")
+    chunks = CAP // (dp_count * TILE)
+    half = dp_count // 2
+    low, high = 1, 4
+    pairs = list(itertools.combinations(range(half), 2))
+    branches = [
+        functools.partial(kernel_device, low, high, (a, b, a + half, b + half), variant)
+        for variant, (a, b) in enumerate(pairs)
+    ]
+    branches.append(
+        functools.partial(kernel_device, 0, chunks, tuple(range(dp_count)), len(pairs))
+    )
+    sets = jnp.array([[(1 << a) | (1 << b)] for a, b in pairs], jnp.int32)
+    place = jnp.left_shift(1, user_owner % half)[None, :]
+    over = (counts > (high - low) * dp_count * TILE)[None, :]
+    misfits = jnp.sum(jnp.where(over & ((place & sets) == 0), 1, 0), axis=1)
+    order = jnp.arange(len(pairs), dtype=jnp.int32)
+    choice = jnp.min(jnp.where(misfits == 0, order, len(pairs)))
+    return lax.switch(
+        choice, branches, new_rows, counts, history_len, user_owner, cache_kv, w_out
+    )
 
 
 def solution(mesh):
     placed = (P(None, "dp", None, "mp"), P(), P(), P(), P("dp", None, None, "mp"), P(None, "mp"))
     fits = mesh.shape["dp"] * TILE == 128
     return jax.shard_map(
-        whole_device if fits else general_device,
+        switched_device if fits else general_device,
         mesh=mesh,
         in_specs=placed,
         out_specs=(P("dp", None, None, "mp"), P("dp", None, "mp")),

time: 70.6 us -> 68.5 us (0.970)
  Pallas kernels: 65 us -> 59.2 us
  other arithmetic: 0 us -> 2.8 us
    pallas_call x1, Pallas kernels: 65 us -> 59.2 us  [kernel_device(): pl.pallas_call(functools.partial(layer_kernel, dp_count, mp_count, low, h...]
    cond x0 -> x12, local copies, waits for them, and re-layouts: none -> 2.57 us
    unnamed x13 -> x1, local copies, waits for them, and re-layouts: 3.33 us -> 0.78 us
    reduce_sum x0 -> x1, other arithmetic: none -> 0.84 us  [switched_device(): misfits = jnp.sum(jnp.where(over & (place & sets == 0), 1, 0), axis=1)]
where the time goes in v5:
time: 68.5 us; the launch traced here: 68.3 us
  Pallas kernels  59.2 us (86%)
  local copies, waits for them, and re-layouts  4.52 us (7%)
  other arithmetic  2.8 us (4%)
  between operations  1.29 us (2%)
    pallas_call x1, Pallas kernels, kernel_device(): pl.pallas_call(functools.partial(layer_kernel, dp_count, mp_count, low, h...  59.2 us
    cond x12, local copies, waits for them, and re-layouts  2.57 us

profile of v5, /device:TPU:11, one launch (start us, length us, event | category | flops | bytes accessed | tf_op | source)
XLA Modules:
  0.0 68.3 jit_solution(560340690607283459)
XLA Ops:
  0.6 0.7 broadcast_compare_fusion
  1.3 0.7 fusion.1
  2.0 0.8 %select_reduce_fusion = s32[6]{0:T(128)S(1)} fusion(s32[6]{0:T(128)} %constant.32, s32[8]{0:T(128)S(1)} %fusion.1, pred[8]{0:T(512)(128)(4,1)S(1)} %broadcast_compare_fusion), kind=kLoop, calls=%fused_computation | loop fusion | flops 234 | bytes 88 | tf_op jit(solution)/shard_map/reduce_sum | solution.py:474
  2.8 0.6 fusion.2
  4.1 62.3 %conditional.1 = ((bf16[640,768]{1,0:T(8,128)(2,1)S(1)}, bf16[640,384]{1,0:T(8,128)(2,1)S(1)})) conditional(s32[]{:T(128)} %clamp.3, (bf16[256,1,4,384]{3,2,1,0:T(4,128)(2,1)}, bf16[1,512,2,384]{3,2,1,0:T(2,128)(2,1)}, s32[8]{0:T(128)}, s32[8]{0:T(128)}, s32[8]{0:T(128)}, ...), branch_computations={%region_2.3_spmd, %region_3.4_spmd, %region_4.5_spmd, %region_5.6_... | conditional | bytes 11010580 | solution.py:477
  4.1 0.0 copy-start.9
  4.1 1.3 %copy.28 = bf16[64,8,2,384]{3,1,2,0:T(8,128)(2,1)S(1)} copy(bf16[64,8,2,384]{3,2,1,0:T(2,128)(2,1)} %bitcast.80) | data formatting | bytes 1572864 | tf_op jit(solution)/shard_map/cond
  5.5 0.0 copy-start.2
  5.5 0.0 copy-start.16
  5.5 0.0 copy-start.23
  5.5 0.0 copy-start.30
  5.5 0.0 copy-done.9
  5.5 0.1 copy.27
  5.6 1.1 %copy-done.2 = bf16[1536,384]{1,0:T(8,128)(2,1)S(1)} copy-done((bf16[1536,384]{1,0:T(8,128)(2,1)S(1)}, bf16[1536,384]{1,0:T(8,128)(2,1)}, u32[]{:S(2)}) %copy-start.2) | copy-done | bytes 1179672 | tf_op jit(solution)/shard_map/cond
  6.7 0.0 copy-done.16
  6.7 0.0 copy-done.23
  6.8 0.0 copy-done.30
  6.8 59.2 %branch_2_fun.1 = (bf16[640,768]{1,0:T(8,128)(2,1)S(1)}, bf16[640,384]{1,0:T(8,128)(2,1)S(1)}) custom-call(s32[8]{0:T(128)S(1)} %copy-done.23, s32[8]{0:T(128)S(1)} %copy-done.30, s32[8]{0:T(128)S(1)} %copy-done.16, bf16[256,1536]{1,0:T(8,128)(2,1)S(1)} %bitcast.62, bf16[512,768]{1,0:T(8,128)(2,1)S(1)} %bitcast.61, bf16[1536,384]{1,0:T(8,128)(2,1)S(1)} %copy-done.2), custom_call_target="tpu_custom_call" | custom-call | tf_op jit(solution)/shard_map/cond/branch_2_fun/pallas_call | solution.py:417
  66.4 1.2 %reshape.69 = bf16[1,640,2,384]{3,2,1,0:T(2,128)(2,1)} reshape(bf16[640,768]{1,0:T(8,128)(2,1)S(1)} %get-tuple-element.144) | data formatting | bytes 1966080 | tf_op jit(solution)/shard_map/cond/branch_0_fun/reshape | solution.py:455
  67.6 0.8 %copy.52 = bf16[1,640,384]{2,1,0:T(8,128)(2,1)} copy(bf16[1,640,384]{2,1,0:T(8,128)(2,1)S(1)} %bitcast.85) | data formatting | bytes 983040
Async XLA Ops:
  4.1 1.4 %copy-start.9 = (bf16[256,1,4,384]{3,2,1,0:T(4,128)(2,1)S(1)}, bf16[256,1,4,384]{3,2,1,0:T(4,128)(2,1)}, u32[]{:S(2)}) copy-start(bf16[256,1,4,384]{3,2,1,0:T(4,128)(2,1)} %get-tuple-element.199) | copy-start | bytes 2359300 | tf_op jit(solution)/shard_map/cond
  5.5 1.3 %copy-start.2 = (bf16[1536,384]{1,0:T(8,128)(2,1)S(1)}, bf16[1536,384]{1,0:T(8,128)(2,1)}, u32[]{:S(2)}) copy-start(bf16[1536,384]{1,0:T(8,128)(2,1)} %get-tuple-element.105.w_ref) | copy-start | bytes 3538948 | tf_op jit(solution)/shard_map/cond
  5.5 1.3 %copy-start.16 = (s32[8]{0:T(128)S(1)}, s32[8]{0:T(128)}, u32[]{:S(2)}) copy-start(s32[8]{0:T(128)} %get-tuple-element.102.owner_ref) | copy-start | bytes 100 | tf_op jit(solution)/shard_map/cond
  5.5 1.3 %copy-start.23 = (s32[8]{0:T(128)S(1)}, s32[8]{0:T(128)}, u32[]{:S(2)}) copy-start(s32[8]{0:T(128)} %get-tuple-element.100.counts_ref) | copy-start | bytes 100 | tf_op jit(solution)/shard_map/cond
  5.5 1.3 %copy-start.30 = (s32[8]{0:T(128)S(1)}, s32[8]{0:T(128)}, u32[]{:S(2)}) copy-start(s32[8]{0:T(128)} %get-tuple-element.101.history_ref) | copy-start | bytes 100 | tf_op jit(solution)/shard_map/cond

commit v6 on v5

--- a/solution.py
+++ b/solution.py
@@ -169,6 +169,43 @@
             device_id_type=pl.DeviceIdType.MESH,
         )
 
+    my_core = lax.rem(my_part, 2)
+    near = my_part + 1 - 2 * my_core
+    far = lax.rem(my_part - my_core + 2, mp_count)
+
+    def gated_copy(c, source, half, index, target):
+        block = gated_buf.at[c, source] if half is None else gated_buf.at[c, source, half]
+        return pltpu.make_async_remote_copy(
+            src_ref=block,
+            dst_ref=block,
+            send_sem=gated_send.at[c, index],
+            recv_sem=gated_recv.at[c, index],
+            device_id=(me, target),
+            device_id_type=pl.DeviceIdType.MESH,
+        )
+
+    def near_copy(c):
+        return gated_copy(c, my_part, None, 0, near)
+
+    def near_arrival(c):
+        return gated_copy(c, near, None, 0, near)
+
+    def far_copy(c, core):
+        return pltpu.make_async_remote_copy(
+            src_ref=gated_buf.at[c, my_part, core],
+            dst_ref=gated_buf.at[c, my_part, core],
+            send_sem=gated_send.at[c, 1 + core],
+            recv_sem=gated_recv.at[c, 1 + my_core],
+            device_id=(me, far + core),
+            device_id_type=pl.DeviceIdType.MESH,
+        )
+
+    def far_arrival(c, core):
+        return gated_copy(c, far + core, my_core, 1 + core, far + core)
+
+    def pass_copy(c, core, half):
+        return gated_copy(c, far + core, half, 3 + core, near)
+
     barrier = pltpu.get_barrier_semaphore()
     for step in range(1, dp_count):
         pl.semaphore_signal(
@@ -329,20 +366,30 @@
         stats = jnp.where(line == 0, mean, lax.rsqrt(variance + EPSILON))
         stats = jnp.concatenate([stats, jnp.zeros((128 - 8, chunk), jnp.float32)], axis=0).T
         normed = (attended_buf[...] - stats[:, 0:1]) * stats[:, 1:2]
-        gated_buf[c, my_part] = (normed * gate_buf[...]).astype(jnp.bfloat16)
-        for step in range(1, mp_count):
-            part_copy(gated_buf, gated_send, gated_recv, c, my_part, part(step)).start()
+        gated = (normed * gate_buf[...]).astype(jnp.bfloat16)
+        gated_buf[c, my_part] = gated.reshape(2, chunk // 2, width)
+        for core in range(2):
+            far_copy(c, core).start()
+        near_copy(c).start()
 
     def mix(c):
-        for step in range(1, mp_count):
-            part_copy(gated_buf, gated_send, gated_recv, c, part(step), my_part).wait_recv()
-        mixed = jnp.zeros((chunk, width), jnp.float32)
-        for index in range(mp_count):
-            mixed = mixed + jnp.dot(
-                gated_buf[c, index],
-                w_buf[index * width : (index + 1) * width, :],
+        def product(source):
+            rows = pl.ds(pl.multiple_of(source * width, width), width)
+            return jnp.dot(
+                gated_buf[c, source].reshape(chunk, width),
+                w_buf[rows, :],
                 preferred_element_type=jnp.float32,
             )
+
+        for core in range(2):
+            far_arrival(c, core).wait_recv()
+            pass_copy(c, core, my_core).start()
+        mixed = product(my_part)
+        near_arrival(c).wait_recv()
+        mixed = mixed + product(near)
+        for core in range(2):
+            pass_copy(c, core, 1 - my_core).wait_recv()
+            mixed = mixed + product(far + core)
         here = pl.ds(pl.multiple_of((c - first_step) * chunk, chunk), chunk)
         live = (c - first_step) * chunk + chunk_row < my_count
         out_ref[here, :] = jnp.where(live, mixed, 0.0).astype(jnp.bfloat16)
@@ -389,7 +436,10 @@
     def finish_parts(c, carry):
         for step in range(1, mp_count):
             part_copy(stats_buf, stats_send, stats_recv, c, my_part, part(step)).wait_send()
-            part_copy(gated_buf, gated_send, gated_recv, c, my_part, part(step)).wait_send()
+        near_copy(c).wait_send()
+        for core in range(2):
+            far_copy(c, core).wait_send()
+            pass_copy(c, core, my_core).wait_send()
         return carry
 
     lax.fori_loop(low, high, finish_parts, 0)
@@ -432,13 +482,13 @@
             pltpu.VMEM((chunk, width), jnp.float32),
             pltpu.VMEM((chunk, width), jnp.float32),
             pltpu.VMEM((chunks, mp_count, 8, chunk), jnp.float32),
-            pltpu.VMEM((chunks, mp_count, chunk, width), jnp.bfloat16),
+            pltpu.VMEM((chunks, mp_count, 2, chunk // 2, width), jnp.bfloat16),
             dma((chunks, dp_count)),
             dma((chunks, dp_count)),
             dma((chunks, mp_count)),
             dma((chunks, mp_count)),
-            dma((chunks, mp_count)),
-            dma((chunks, mp_count)),
+            dma((chunks, 5)),
+            dma((chunks, 5)),
             dma,
         ],
         compiler_params=pltpu.CompilerParams(
@@ -455,6 +505,22 @@
     return (key_value.reshape(1, CAP, 2, width), results[None])
 
 
+def choice_kernel(pairs, half, limit, counts_ref, owner_ref, choice_ref):
+    fits = [jnp.bool_(True)] * len(pairs)
+    for user in range(counts_ref.shape[0]):
+        small = counts_ref[user] <= limit
+        place = lax.rem(owner_ref[user], half)
+        held = [jnp.logical_or(small, place == index) for index in range(half)]
+        fits = [
+            jnp.logical_and(fit, jnp.logical_or(held[a], held[b]))
+            for fit, (a, b) in zip(fits, pairs)
+        ]
+    choice = jnp.int32(len(pairs))
+    for variant, fit in enumerate(fits):
+        choice = jnp.where(fit, jnp.int32(variant), choice)
+    choice_ref[0] = choice
+
+
 def switched_device(new_rows, counts, history_len, user_owner, cache_kv, w_out):
     dp_count = lax.axis_size("dp")
     chunks = CAP // (dp_count * TILE)
@@ -468,12 +534,13 @@
     branches.append(
         functools.partial(kernel_device, 0, chunks, tuple(range(dp_count)), len(pairs))
     )
-    sets = jnp.array([[(1 << a) | (1 << b)] for a, b in pairs], jnp.int32)
-    place = jnp.left_shift(1, user_owner % half)[None, :]
-    over = (counts > (high - low) * dp_count * TILE)[None, :]
-    misfits = jnp.sum(jnp.where(over & ((place & sets) == 0), 1, 0), axis=1)
-    order = jnp.arange(len(pairs), dtype=jnp.int32)
-    choice = jnp.min(jnp.where(misfits == 0, order, len(pairs)))
+    smem = pl.BlockSpec(memory_space=pltpu.SMEM)
+    choice = pl.pallas_call(
+        functools.partial(choice_kernel, pairs, half, (high - low) * dp_count * TILE),
+        out_shape=jax.ShapeDtypeStruct((1,), jnp.int32),
+        in_specs=[smem, smem],
+        out_specs=smem,
+    )(counts, user_owner)[0]
     return lax.switch(
         choice, branches, new_rows, counts, history_len, user_owner, cache_kv, w_out
     )
@@ -481,7 +548,7 @@
 
 def solution(mesh):
     placed = (P(None, "dp", None, "mp"), P(), P(), P(), P("dp", None, None, "mp"), P(None, "mp"))
-    fits = mesh.shape["dp"] * TILE == 128
+    fits = mesh.shape["dp"] * TILE == 128 and mesh.shape["mp"] == 4
     return jax.shard_map(
         switched_device if fits else general_device,
         mesh=mesh,

time: 68.5 us -> 63 us (0.920)
  Pallas kernels: 59.2 us -> 56.2 us
  other arithmetic: 2.8 us -> 0 us
    pallas_call x1, Pallas kernels: 59.2 us -> 54.9 us  [kernel_device(): pl.pallas_call(functools.partial(layer_kernel, dp_count, mp_count, low, h...]
    pallas_call x0 -> x1, Pallas kernels: none -> 1.32 us  [switched_device(): pl.pallas_call(functools.partial(choice_kernel, pairs, half, (high - low)...]
    reduce_sum x1 -> x0, other arithmetic: 0.84 us -> none  [switched_device(): misfits = jnp.sum(jnp.where(over & (place & sets == 0), 1, 0), axis=1)]
where the time goes in v6:
time: 63 us; the launch traced here: 62.6 us
  Pallas kernels  56.2 us (89%)
  local copies, waits for them, and re-layouts  4.52 us (7%)
  between operations  1.29 us (2%)
  loops' own time  0.63 us (1%)
    pallas_call x1, Pallas kernels, kernel_device(): pl.pallas_call(functools.partial(layer_kernel, dp_count, mp_count, low, h...  54.9 us
    cond x12, local copies, waits for them, and re-layouts  2.57 us
    pallas_call x1, Pallas kernels, switched_device(): pl.pallas_call(functools.partial(choice_kernel, pairs, half, (high - low)...  1.32 us

profile of v6, /device:TPU:11, one launch (start us, length us, event | category | flops | bytes accessed | tf_op | source)
XLA Modules:
  0.0 62.6 jit_solution(9411807015876207929)
XLA Ops:
  0.6 1.3 %shard_map.77 = s32[1]{0:T(128)} custom-call(s32[8]{0:T(128)} %counts_ref.1, s32[8]{0:T(128)} %owner_ref.1), custom_call_target="tpu_custom_call" | custom-call | tf_op jit(solution)/shard_map/pallas_call | solution.py:538
  2.6 58.1 %conditional.1 = ((bf16[640,768]{1,0:T(8,128)(2,1)S(1)}, bf16[640,384]{1,0:T(8,128)(2,1)S(1)})) conditional(s32[]{:T(128)} %bitcast.7, (bf16[256,1,4,384]{3,2,1,0:T(4,128)(2,1)}, bf16[1,512,2,384]{3,2,1,0:T(2,128)(2,1)}, s32[8]{0:T(128)}, s32[8]{0:T(128)}, s32[8]{0:T(128)}, ...), branch_computations={%region_0.0_spmd, %region_1.0_spmd, %region_2.0_spmd, %region_3.0_... | conditional | bytes 11010580 | solution.py:544
  2.6 0.0 copy-start.9
  2.7 1.3 %copy.20 = bf16[64,8,2,384]{3,1,2,0:T(8,128)(2,1)S(1)} copy(bf16[64,8,2,384]{3,2,1,0:T(2,128)(2,1)} %bitcast.81) | data formatting | bytes 1572864 | tf_op jit(solution)/shard_map/cond
  4.0 0.0 copy-start.2
  4.0 0.0 copy-start.16
  4.0 0.0 copy-start.23
  4.0 0.0 copy-start.30
  4.0 0.0 copy-done.9
  4.0 0.1 copy.19
  4.2 1.1 %copy-done.2 = bf16[1536,384]{1,0:T(8,128)(2,1)S(1)} copy-done((bf16[1536,384]{1,0:T(8,128)(2,1)S(1)}, bf16[1536,384]{1,0:T(8,128)(2,1)}, u32[]{:S(2)}) %copy-start.2) | copy-done | bytes 1179672 | tf_op jit(solution)/shard_map/cond
  5.3 0.0 copy-done.16
  5.3 0.0 copy-done.23
  5.3 0.0 copy-done.30
  5.3 54.9 %branch_2_fun.1 = (bf16[640,768]{1,0:T(8,128)(2,1)S(1)}, bf16[640,384]{1,0:T(8,128)(2,1)S(1)}) custom-call(s32[8]{0:T(128)S(1)} %copy-done.16, s32[8]{0:T(128)S(1)} %copy-done.30, s32[8]{0:T(128)S(1)} %copy-done.23, bf16[256,1536]{1,0:T(8,128)(2,1)S(1)} %bitcast.63, bf16[512,768]{1,0:T(8,128)(2,1)S(1)} %bitcast.62, bf16[1536,384]{1,0:T(8,128)(2,1)S(1)} %copy-done.2), custom_call_target="tpu_custom_call" | custom-call | tf_op jit(solution)/shard_map/cond/branch_2_fun/pallas_call | solution.py:467
  60.7 1.2 %reshape.70 = bf16[1,640,2,384]{3,2,1,0:T(2,128)(2,1)} reshape(bf16[640,768]{1,0:T(8,128)(2,1)S(1)} %get-tuple-element.144) | data formatting | bytes 1966080 | tf_op jit(solution)/shard_map/cond/branch_0_fun/reshape | solution.py:505
  61.8 0.8 %copy.44 = bf16[1,640,384]{2,1,0:T(8,128)(2,1)} copy(bf16[1,640,384]{2,1,0:T(8,128)(2,1)S(1)} %bitcast.86) | data formatting | bytes 983040
Async XLA Ops:
  2.6 1.4 %copy-start.9 = (bf16[256,1,4,384]{3,2,1,0:T(4,128)(2,1)S(1)}, bf16[256,1,4,384]{3,2,1,0:T(4,128)(2,1)}, u32[]{:S(2)}) copy-start(bf16[256,1,4,384]{3,2,1,0:T(4,128)(2,1)} %get-tuple-element.157) | copy-start | bytes 2359300 | tf_op jit(solution)/shard_map/cond
  4.0 1.3 %copy-start.2 = (bf16[1536,384]{1,0:T(8,128)(2,1)S(1)}, bf16[1536,384]{1,0:T(8,128)(2,1)}, u32[]{:S(2)}) copy-start(bf16[1536,384]{1,0:T(8,128)(2,1)} %get-tuple-element.105.w_ref) | copy-start | bytes 3538948 | tf_op jit(solution)/shard_map/cond
  4.0 1.3 %copy-start.16 = (s32[8]{0:T(128)S(1)}, s32[8]{0:T(128)}, u32[]{:S(2)}) copy-start(s32[8]{0:T(128)} %get-tuple-element.100.counts_ref) | copy-start | bytes 100 | tf_op jit(solution)/shard_map/cond
  4.0 1.3 %copy-start.23 = (s32[8]{0:T(128)S(1)}, s32[8]{0:T(128)}, u32[]{:S(2)}) copy-start(s32[8]{0:T(128)} %get-tuple-element.102.owner_ref) | copy-start | bytes 100 | tf_op jit(solution)/shard_map/cond
  4.0 1.3 %copy-start.30 = (s32[8]{0:T(128)S(1)}, s32[8]{0:T(128)}, u32[]{:S(2)}) copy-start(s32[8]{0:T(128)} %get-tuple-element.101.history_ref) | copy-start | bytes 100 | tf_op jit(solution)/shard_map/cond
